TPU v7x, 32 devices: a whole 2x2x4 slice. The times are simulated.
32 devices in a mesh: ev: 8 (over z, x), node: 4 (over y, core).
Axes of the slice: x: 2, y: 2, z: 4, core: 2. Of those that a mesh axis runs over, the one named last changes fastest.
Arguments:
- src_owner: int32 [16384, 1], P(('ev', 'node')), may hold values from 0 to 31; in each aligned block of 512 rows (0 to 511, 512 to 1023, ...) at most 32 rows name the same one
- src_row: int32 [16384], P(('ev', 'node')), may hold values from 0 to 4095
- dst_owner: int32 [16384, 1], P(('ev', 'node')), may hold values from 0 to 31; in each aligned block of 512 rows (0 to 511, 512 to 1023, ...) at most 32 rows name the same one
- dst_row: int32 [16384], P(('ev', 'node')), may hold values from 0 to 4095
- event_time: int32 [16384], P(('ev', 'node')), may hold values from 4096 to 8191
- edge_feat: bfloat16 [16384, 256], P(('ev', 'node')), may hold values from -6 to 6
- memory: bfloat16 [131072, 256], P(('ev', 'node')), may hold values from -3 to 3
- last_update: int32 [131072], P(('ev', 'node')), may hold values from 0 to 4095
- time_freq: float32 [128], replicated, may hold values from 0.0001 to 1
- time_phase: float32 [128], replicated, may hold values from -3.140625 to 3.140625
- w_msg_in: bfloat16 [896, 512], replicated, may hold values from -0.1875 to 0.1875
- b_msg: float32 [512], replicated, may hold values from -3 to 3
- w_msg_out: bfloat16 [512, 256], replicated, may hold values from -0.25 to 0.25
- w_gru_in: bfloat16 [256, 768], replicated, may hold values from -0.375 to 0.375
- b_gru_in: float32 [768], replicated, may hold values from -3 to 3
- w_gru_hid: bfloat16 [256, 768], replicated, may hold values from -0.375 to 0.375
Outputs:
- new_memory: bfloat16 [131072, 256], P(('ev', 'node'))
Inputs may be any that keep to these rules, and one draw needn't show every extreme that they name: `src_owner`: within the events of one device (aligned blocks of 512 rows) no owner is named by more than 32 events, a bound that some block reaches. `dst_owner`: within the events of one device (aligned blocks of 512 rows) no owner is named by more than 32 events, a bound that some block reaches. `event_time`: every event is later than the last update of either of its nodes.
All inputs are finite; a program needn't handle non-finite values.
Results may differ from a plain program's by a relative error of at most 0.0021.
Values may be sent and summed in bfloat16 or wider, within the bound.
A program may use at most 64 MiB of HBM per device.

v0:
```python
import jax
import jax.numpy as jnp
from jax import lax
from jax.sharding import PartitionSpec as P


def encode(delta_int, time_freq, time_phase):
    delta = delta_int.astype(jnp.float32)
    return jnp.cos(delta[..., None] * time_freq + time_phase).astype(jnp.bfloat16)


def gru_update(mean_msg, state, w_gru_in, b_gru_in, w_gru_hid):
    width = state.shape[-1]
    input_part = jnp.dot(mean_msg, w_gru_in, preferred_element_type=jnp.float32) + b_gru_in
    state_part = jnp.dot(state, w_gru_hid, preferred_element_type=jnp.float32)
    reset = jax.nn.sigmoid(input_part[:, :width] + state_part[:, :width])
    update = jax.nn.sigmoid(input_part[:, width : 2 * width] + state_part[:, width : 2 * width])
    candid = jnp.tanh(input_part[:, 2 * width :] + reset * state_part[:, 2 * width :])
    return ((1.0 - update) * candid + update * state.astype(jnp.float32)).astype(jnp.bfloat16)


def slot_of(owner_ids, owner_count, capacity):
    events_here = owner_ids.shape[0]
    columns = jnp.arange(owner_count, dtype=jnp.int32)
    onehot = (owner_ids[:, None] == columns[None, :]).astype(jnp.bfloat16)
    order = jnp.arange(events_here, dtype=jnp.int32)
    lower = (order[None, :] < order[:, None]).astype(jnp.bfloat16)
    earlier = jnp.dot(lower, onehot, preferred_element_type=jnp.float32)
    position = jnp.sum(earlier * onehot.astype(jnp.float32), axis=1).astype(jnp.int32)
    return owner_ids * capacity + position


def owner_lookup(request_pair, memory, last_update, time_freq, time_phase):
    row_request = request_pair[0]
    time_request = request_pair[1]
    safe_rows = jnp.clip(row_request, 0, memory.shape[0] - 1)
    mem_rows = memory[safe_rows]
    encoded = encode(time_request - last_update[safe_rows], time_freq, time_phase)
    return jnp.concatenate([mem_rows, encoded], axis=-1)


def local(
    src_owner,
    src_row,
    dst_owner,
    dst_row,
    event_time,
    edge_feat,
    memory,
    last_update,
    time_freq,
    time_phase,
    w_msg_in,
    b_msg,
    w_msg_out,
    w_gru_in,
    b_gru_in,
    w_gru_hid,
):
    devices_all = lax.axis_size(("ev", "node"))
    events_here = edge_feat.shape[0]
    capacity = max(2, 2 * events_here // devices_all)
    width = memory.shape[1]
    time_width = time_freq.shape[0]
    hidden_width = w_msg_out.shape[0]
    msg_width = w_msg_out.shape[1]
    rows_count = memory.shape[0]
    slot_total = devices_all * capacity
    slot_ids = jnp.stack(
        [
            slot_of(src_owner[:, 0], devices_all, capacity),
            slot_of(dst_owner[:, 0], devices_all, capacity),
        ]
    )
    slot_range = jnp.arange(slot_total, dtype=jnp.int32)
    placed = slot_ids[:, None, :] == slot_range[None, :, None]
    placement = placed.astype(jnp.bfloat16)
    filled = jnp.any(placed, axis=2)
    rows_pair = jnp.stack([src_row, dst_row])
    row_sum = jnp.sum(jnp.where(placed, rows_pair[:, None, :], 0), axis=2)
    time_sum = jnp.sum(jnp.where(placed, event_time[None, None, :], 0), axis=2)
    row_request = jnp.where(filled, row_sum, -1)
    time_request = jnp.where(filled, time_sum, 0)
    edge_part = (
        jnp.dot(edge_feat, w_msg_in[2 * width + time_width :], preferred_element_type=jnp.float32)
        + b_msg
    )
    flat_shape = (2, devices_all, capacity)
    received = (
        lax.all_to_all(
            row_request.reshape(flat_shape), ("ev", "node"), split_axis=1, concat_axis=1, tiled=True
        ),
        lax.all_to_all(
            time_request.reshape(flat_shape),
            ("ev", "node"),
            split_axis=1,
            concat_axis=1,
            tiled=True,
        ),
    )
    served = owner_lookup(received, memory, last_update, time_freq, time_phase)
    returned = lax.all_to_all(served, ("ev", "node"), split_axis=1, concat_axis=1, tiled=True)
    rows_held = received[0]
    fetched_flat = returned.reshape(2, slot_total, width + time_width)
    picked = jnp.einsum(
        "kse,ksc->kec", placement, fetched_flat, preferred_element_type=jnp.float32
    ).astype(jnp.bfloat16)
    picked_src = picked[0]
    picked_dst = picked[1]
    mem_stack = jnp.concatenate([picked_src[:, :width], picked_dst[:, :width]], axis=0)
    enc_stack = jnp.concatenate([picked_src[:, width:], picked_dst[:, width:]], axis=0)
    paired_weight = jnp.concatenate([w_msg_in[:width], w_msg_in[width : 2 * width]], axis=1)
    projected = jnp.dot(mem_stack, paired_weight, preferred_element_type=jnp.float32)
    time_term = jnp.dot(
        enc_stack, w_msg_in[2 * width : 2 * width + time_width], preferred_element_type=jnp.float32
    )
    self_term = projected[:, :hidden_width]
    other_term = projected[:, hidden_width:]
    crossed = jnp.concatenate([other_term[events_here:], other_term[:events_here]], axis=0)
    edge_both = jnp.concatenate([edge_part, edge_part], axis=0)
    hidden = jax.nn.relu(self_term + crossed + time_term + edge_both).astype(jnp.bfloat16)
    messages = jnp.dot(hidden, w_msg_out, preferred_element_type=jnp.float32).astype(jnp.bfloat16)
    outgoing = jnp.einsum(
        "kse,kec->ksc",
        placement,
        messages.reshape(2, events_here, msg_width),
        preferred_element_type=jnp.float32,
    ).astype(jnp.bfloat16)
    arrived = lax.all_to_all(
        outgoing.reshape(2, devices_all, capacity, msg_width),
        ("ev", "node"),
        split_axis=1,
        concat_axis=1,
        tiled=True,
    )
    row_flat = rows_held.reshape(-1)
    msg_flat = arrived.reshape(-1, msg_width)
    live = row_flat >= 0
    same_row = (row_flat[:, None] == row_flat[None, :]) & live[:, None] & live[None, :]
    same_mask = same_row.astype(jnp.bfloat16)
    total = jnp.dot(same_mask, msg_flat, preferred_element_type=jnp.float32)
    count = jnp.sum(same_mask.astype(jnp.float32), axis=1)
    divisor = jnp.maximum(count, 1.0)
    mean_msg = (total / divisor[:, None]).astype(jnp.bfloat16)
    safe_rows = jnp.clip(row_flat, 0, rows_count - 1)
    new_state = gru_update(mean_msg, memory[safe_rows], w_gru_in, b_gru_in, w_gru_hid)
    slot_order = jnp.arange(row_flat.shape[0], dtype=jnp.int32)
    before = slot_order[None, :] < slot_order[:, None]
    repeated = jnp.any(same_row & before, axis=1)
    first_live = live & jnp.logical_not(repeated)
    row_range = jnp.arange(rows_count, dtype=jnp.int32)
    writes = (row_range[:, None] == row_flat[None, :]) & first_live[None, :]
    write_mask = writes.astype(jnp.bfloat16)
    written = jnp.dot(write_mask, new_state, preferred_element_type=jnp.float32).astype(
        jnp.bfloat16
    )
    touched = jnp.any(writes, axis=1)
    return jnp.where(touched[:, None], written, memory)


def solution(mesh):
    in_specs = (
        P(("ev", "node"), None),
        P(("ev", "node")),
        P(("ev", "node"), None),
        P(("ev", "node")),
        P(("ev", "node")),
        P(("ev", "node"), None),
        P(("ev", "node"), None),
        P(("ev", "node")),
        P(),
        P(),
        P(),
        P(),
        P(),
        P(),
        P(),
        P(),
    )
    out_specs = P(("ev", "node"), None)
    return jax.shard_map(local, mesh=mesh, in_specs=in_specs, out_specs=out_specs, check_vma=False)
```

profile of v0, /device:TPU:0, one launch (start us, length us, event | category | flops | bytes accessed | tf_op | source)
XLA Modules:
  0.0 165.9 jit_solution(13599117809676873380)
XLA Ops:
  4.0 2.0 %select_reduce_fusion = (s32[2,1024]{1,0:T(2,128)S(1)}, s32[2,1024]{1,0:T(2,128)S(1)}) fusion(s32[512]{0:T(512)} %param.20, s32[2,512]{1,0:T(2,128)S(1)} %pad_add_fusion, s32[2,512]{1,0:T(2,128)S(1)} %pad_add_fusion.1), kind=kLoop, calls=%fused_computation.22 | loop fusion | flops 5238784 | bytes 26624 | tf_op jit(solution)/shard_map/reduce_sum | solution.py:81
  6.8 7.3 %all-to-all-start = ((s32[2,32,32]{2,0,1:T(2,128)}), s32[2,32,32]{2,0,1:T(2,128)S(1)}, u32[]{:S(2)}, u32[]{:S(2)}) async-start(s32[2,32,32]{2,0,1:T(2,128)} %copy.35), calls=%async_computation | async-start | bytes 65536 | tf_op jit(solution)/shard_map/all_to_all | solution.py:90
  14.8 6.5 %all-to-all-done = s32[2,32,32]{2,0,1:T(2,128)S(1)} async-done(((s32[2,32,32]{2,0,1:T(2,128)}), s32[2,32,32]{2,0,1:T(2,128)S(1)}, u32[]{:S(2)}, u32[]{:S(2)}) %all-to-all-start) | async-done | bytes 8224 | tf_op jit(solution)/shard_map/all_to_all | solution.py:90
  21.4 2.6 %all-to-all-start.1 = ((s32[2,32,32]{2,0,1:T(2,128)}), s32[2,32,32]{2,0,1:T(2,128)S(1)}, u32[]{:S(2)}, u32[]{:S(2)}) async-start(s32[2,32,32]{2,0,1:T(2,128)} %copy.38), calls=%async_computation.1 | async-start | bytes 65536 | tf_op jit(solution)/shard_map/all_to_all | solution.py:93
  24.7 11.8 %gather_fusion.1 = s32[2048]{0:T(1024)S(1)} fusion(s32[4096]{0:T(1024)S(1)} %copy-done.1, s32[2048]{0:T(1024)S(1)} %broadcast_clamp_fusion.2), kind=kCustom, calls=%fused_computation.1 | custom fusion | bytes 24576 | tf_op jit(solution)/shard_map/gather | solution.py:38
  37.2 7.5 %gather_fusion = bf16[2048,256]{1,0:T(8,128)(2,1)S(1)} fusion(bf16[4096,256]{1,0:T(8,128)(2,1)S(1)} %copy-done.2, s32[2048]{0:T(1024)S(1)} %broadcast_clamp_fusion.2), kind=kCustom, calls=%fused_computation | custom fusion | bytes 2105344 | tf_op jit(solution)/shard_map/gather | solution.py:37
  44.7 4.5 %cosine_convert_fusion = bf16[2,32,32,128]{3,2,0,1:T(8,128)(2,1)S(1)} fusion(f32[128]{0:T(128)S(1)} %copy-done.13, f32[128]{0:T(128)} %param.24, f32[2,32,32]{2,0,1:T(2,128)} %copy.40), kind=kLoop, calls=%fused_computation.65 | loop fusion | flops 786432 | bytes 533504 | tf_op jit(solution)/shard_map/convert_element_type | solution.py:9
  50.6 5.9 %all-to-all-start.2 = ((bf16[2,32,32,384]{3,2,0,1:T(8,128)(2,1)}), bf16[2,32,32,384]{3,2,0,1:T(8,128)(2,1)}, u32[]{:S(2)}, u32[]{:S(2)}) async-start(bf16[2,32,32,384]{3,2,0,1:T(8,128)(2,1)} %pad_maximum_fusion), calls=%async_computation.2 | async-start | bytes 3145728 | tf_op jit(solution)/shard_map/all_to_all | solution.py:102
  56.5 1.9 %fusion.79 = (bf16[256,512]{1,0:T(8,128)(2,1)}, bf16[256,512]{1,0:T(8,128)(2,1)}) fusion(bf16[896,512]{1,0:T(8,128)(2,1)} %param.26), kind=kLoop, calls=%fused_computation.109 | loop fusion | bytes 1048576 | tf_op jit(solution)/shard_map/slice | solution.py:112
  58.4 2.2 %convolution_add_fusion.1 = f32[512,512]{1,0:T(8,128)} fusion(bf16[512,256]{1,0:T(8,128)(2,1)S(1)} %copy-done.8, f32[512]{0:T(512)S(1)} %copy-done.10, bf16[896,512]{1,0:T(8,128)(2,1)} %param.26), kind=kOutput, calls=%fused_computation.56 | convolution fusion | flops 134479872 | bytes 1574912 | tf_op jit(solution)/shard_map/dot_general | solution.py:85
  61.4 8.5 %gather_fusion.2 = bf16[2048,256]{1,0:T(8,128)(2,1)S(1)} fusion(bf16[4096,256]{1,0:T(8,128)(2,1)S(1)} %copy-done.2, s32[2048]{0:T(1024)} %broadcast_clamp_fusion.1), kind=kCustom, calls=%fused_computation.2 | custom fusion | bytes 2105344 | tf_op jit(solution)/shard_map/gather | solution.py:146
  69.9 7.1 %fusion.6 = pred[2048]{0:T(1024)(128)(4,1)} fusion(s32[2048]{0:T(1024)S(1)} %eq.83, pred[2048]{0:T(1024)(128)(4,1)S(1)} %broadcast_compare_fusion), kind=kLoop, calls=%fused_computation.11 | loop fusion | flops 25163776 | bytes 12288 | tf_op jit(solution)/shard_map/reduce_or | solution.py:149
  77.0 17.0 %all-to-all-done.2 = bf16[2,32,32,384]{3,2,0,1:T(8,128)(2,1)} async-done(((bf16[2,32,32,384]{3,2,0,1:T(8,128)(2,1)}), bf16[2,32,32,384]{3,2,0,1:T(8,128)(2,1)}, u32[]{:S(2)}, u32[]{:S(2)}) %all-to-all-start.2) | async-done | bytes 1572896 | tf_op jit(solution)/shard_map/all_to_all | solution.py:102
  99.1 1.9 %copy-done.3 = f32[1024,1024]{1,0:T(8,128)} copy-done((f32[1024,1024]{1,0:T(8,128)}, f32[1024,1024]{1,0:T(8,128)S(1)}, u32[]{:S(2)}) %copy-start.3) | copy-done | bytes 4194328
  102.6 4.6 %fusion.45 = bf16[1024,256]{1,0:T(8,128)(2,1)} fusion(bf16[512,256]{1,0:T(8,128)(2,1)} %param.28, f32[1024,1024]{1,0:T(8,128)} %copy-done.3, f32[512,512]{1,0:T(8,128)} %get-tuple-element.8, f32[512,512]{1,0:T(8,128)} %get-tuple-element.7, f32[512,512]{1,0:T(8,128)} %convolution_add_fusion.1, bf16[512,128]{1,0:T(8,128)(2,1)} %slice.93, ...), kind=kOutput, calls=%fused_computation.58 | convolution fusion | flops 407109632 | bytes 6422528 | tf_op jit(solution)/shard_map/dot_general | solution.py:122
  107.2 1.8 %fusion.42 = bf16[2,1024,256]{2,1,0:T(8,128)(2,1)S(1)} fusion(bf16[2,512,256]{2,1,0:T(8,128)(2,1)} %bitcast.39, s32[2,512]{1,0:T(2,128)S(1)} %pad_add_fusion), kind=kOutput, calls=%fused_computation.54 | convolution fusion | flops 538443776 | bytes 1576960 | tf_op jit(solution)/shard_map/kse,kec->ksc/dot_general | solution.py:123
  110.1 4.0 %all-to-all-start.3 = ((bf16[2,32,32,256]{3,2,0,1:T(8,128)(2,1)}), bf16[2,32,32,256]{3,2,0,1:T(8,128)(2,1)}, u32[]{:S(2)}, u32[]{:S(2)}) async-start(bf16[2,32,32,256]{3,2,0,1:T(8,128)(2,1)} %copy.44), calls=%async_computation.3 | async-start | bytes 2097152 | tf_op jit(solution)/shard_map/all_to_all | solution.py:129
  114.8 4.3 %convert_reduce_fusion = f32[2048]{0:T(1024)S(1)} fusion(s32[2048]{0:T(1024)S(1)} %eq.83, pred[2048]{0:T(1024)(128)(4,1)S(1)} %broadcast_compare_fusion), kind=kLoop, calls=%fused_computation.7 | loop fusion | flops 25163776 | bytes 18432 | tf_op jit(solution)/shard_map/reduce_sum | solution.py:142
  119.1 3.6 %fusion.80 = f32[2048,768]{1,0:T(8,128)} fusion(bf16[2048,256]{1,0:T(8,128)(2,1)S(1)} %gather_fusion.2, bf16[256,768]{1,0:T(8,128)(2,1)S(1)} %copy-done), kind=kOutput, calls=%fused_computation.110 | convolution fusion | flops 805306368 | bytes 7733248 | tf_op jit(solution)/shard_map/dot_general | solution.py:15
  122.8 5.1 %fusion.3 = pred[4096]{0:T(1024)(128)(4,1)} fusion(s32[2048]{0:T(1024)S(1)} %eq.83, pred[2048]{0:T(1024)(128)(4,1)S(1)} %not_and_fusion), kind=kLoop, calls=%fused_computation.6 | loop fusion | flops 25161728 | bytes 14336 | tf_op jit(solution)/shard_map/reduce_or | solution.py:157
  127.8 12.3 %all-to-all-done.3 = bf16[2,32,32,256]{3,2,0,1:T(8,128)(2,1)} async-done(((bf16[2,32,32,256]{3,2,0,1:T(8,128)(2,1)}), bf16[2,32,32,256]{3,2,0,1:T(8,128)(2,1)}, u32[]{:S(2)}, u32[]{:S(2)}) %all-to-all-start.3) | async-done | bytes 1048608 | tf_op jit(solution)/shard_map/all_to_all | solution.py:129
  140.1 2.3 %copy.45 = bf16[2,32,32,256]{3,2,1,0:T(8,128)(2,1)} copy(bf16[2,32,32,256]{3,2,0,1:T(8,128)(2,1)} %all-to-all-done.3) | data formatting | bytes 2097152 | tf_op jit(solution)/shard_map/all_to_all | solution.py:129
  142.4 8.4 %convolution_add_fusion = f32[2048,768]{1,0:T(8,128)} fusion(bf16[256,768]{1,0:T(8,128)(2,1)} %param.29, f32[768]{0:T(1024)} %param.30, bf16[2048,256]{1,0:T(8,128)(2,1)} %bitcast.30, s32[2048]{0:T(1024)S(1)} %eq.83, pred[2048]{0:T(1024)(128)(4,1)} %copy-done.11, f32[2048]{0:T(1024)S(1)} %broadcast_maximum_fusion), kind=kOutput, calls=%fused_computation.28 | convolution fusion | flops 2967994368 | bytes 7754752 | tf_op jit(solution)/shard_map/dot_general | solution.py:14
  150.8 15.1 %fusion.17 = bf16[4096,256]{1,0:T(8,128)(2,1)} fusion(bf16[4096,256]{1,0:T(8,128)(2,1)S(1)} %copy-done.2, s32[2048]{0:T(1024)S(1)} %eq.83, pred[2048]{0:T(1024)(128)(4,1)} %copy-done.12, pred[4096]{0:T(1024)(128)(4,1)} %fusion.3, f32[2048,768]{1,0:T(8,128)} %fusion.80, f32[2048,768]{1,0:T(8,128)} %convolution_add_fusion, bf16[2048,256]{1,0:T(8,128)(2,1)S(1)} %gather_fusion.2), kind=kOutput, calls=%fused_computation.21 | convolution fusion | flops 4322230272 | bytes 17840128 | tf_op jit(solution)/shard_map/dot_general | solution.py:154
  (68 shorter events, 17.4 us)
Async XLA Ops:
  0.0 119.1 %copy-start = (bf16[256,768]{1,0:T(8,128)(2,1)S(1)}, bf16[256,768]{1,0:T(8,128)(2,1)}, u32[]{:S(2)}) copy-start(bf16[256,768]{1,0:T(8,128)(2,1)} %param.31) | copy-start | bytes 1179652
  0.0 24.7 %copy-start.1 = (s32[4096]{0:T(1024)S(1)}, s32[4096]{0:T(1024)}, u32[]{:S(2)}) copy-start(s32[4096]{0:T(1024)} %param.23) | copy-start | bytes 49156
  6.8 14.6 %all-to-all-start = ((s32[2,32,32]{2,0,1:T(2,128)}), s32[2,32,32]{2,0,1:T(2,128)S(1)}, u32[]{:S(2)}, u32[]{:S(2)}) async-start(s32[2,32,32]{2,0,1:T(2,128)} %copy.35), calls=%async_computation | async-start | bytes 65536 | tf_op jit(solution)/shard_map/all_to_all | solution.py:90
  21.4 3.3 %copy-start.6 = (s32[2,32,32]{2,0,1:T(2,128)}, s32[2,32,32]{2,0,1:T(2,128)S(1)}, u32[]{:S(2)}) copy-start(s32[2,32,32]{2,0,1:T(2,128)S(1)} %all-to-all-done) | copy-start | bytes 24580
  21.4 15.2 %all-to-all-start.1 = ((s32[2,32,32]{2,0,1:T(2,128)}), s32[2,32,32]{2,0,1:T(2,128)S(1)}, u32[]{:S(2)}, u32[]{:S(2)}) async-start(s32[2,32,32]{2,0,1:T(2,128)} %copy.38), calls=%async_computation.1 | async-start | bytes 65536 | tf_op jit(solution)/shard_map/all_to_all | solution.py:93
  24.7 12.5 %copy-start.2 = (bf16[4096,256]{1,0:T(8,128)(2,1)S(1)}, bf16[4096,256]{1,0:T(8,128)(2,1)}, u32[]{:S(2)}) copy-start(bf16[4096,256]{1,0:T(8,128)(2,1)} %param.22) | copy-start | bytes 6291460
  37.2 7.5 %copy-start.13 = (f32[128]{0:T(128)S(1)}, f32[128]{0:T(128)}, u32[]{:S(2)}) copy-start(f32[128]{0:T(128)} %param.25) | copy-start | bytes 1540
  44.7 13.7 %copy-start.10 = (f32[512]{0:T(512)S(1)}, f32[512]{0:T(512)}, u32[]{:S(2)}) copy-start(f32[512]{0:T(512)} %param.27) | copy-start | bytes 6148
  50.6 7.8 %copy-start.8 = (bf16[512,256]{1,0:T(8,128)(2,1)S(1)}, bf16[512,256]{1,0:T(8,128)(2,1)}, u32[]{:S(2)}) copy-start(bf16[512,256]{1,0:T(8,128)(2,1)} %param.21) | copy-start | bytes 786436
  50.6 10.0 %copy-start.7 = (s32[2,32,32]{2,0,1:T(2,128)S(1)}, s32[2,32,32]{2,0,1:T(2,128)}, u32[]{:S(2)}) copy-start(s32[2,32,32]{2,0,1:T(2,128)} %copy-done.6) | copy-start | bytes 24580
  50.6 10.1 %copy-start.9 = (s32[2,32,32]{2,0,1:T(2,128)S(1)}, s32[2,32,32]{2,0,1:T(2,128)}, u32[]{:S(2)}) copy-start(s32[2,32,32]{2,0,1:T(2,128)} %get-tuple-element.14) | copy-start | bytes 24580
  50.6 43.5 %all-to-all-start.2 = ((bf16[2,32,32,384]{3,2,0,1:T(8,128)(2,1)}), bf16[2,32,32,384]{3,2,0,1:T(8,128)(2,1)}, u32[]{:S(2)}, u32[]{:S(2)}) async-start(bf16[2,32,32,384]{3,2,0,1:T(8,128)(2,1)} %pad_maximum_fusion), calls=%async_computation.2 | async-start | bytes 3145728 | tf_op jit(solution)/shard_map/all_to_all | solution.py:102
  69.9 44.9 %copy-start.11 = (pred[2048]{0:T(1024)(128)(4,1)}, pred[2048]{0:T(1024)(128)(4,1)S(1)}, u32[]{:S(2)}) copy-start(pred[2048]{0:T(1024)(128)(4,1)S(1)} %broadcast_compare_fusion) | copy-start | bytes 6148
  95.6 2.8 %copy-start.4 = (bf16[256,512]{1,0:T(8,128)(2,1)S(1)}, bf16[256,512]{1,0:T(8,128)(2,1)}, u32[]{:S(2)}) copy-start(bf16[256,512]{1,0:T(8,128)(2,1)} %get-tuple-element.9) | copy-start | bytes 786436
  95.6 2.8 %copy-start.5 = (bf16[256,512]{1,0:T(8,128)(2,1)S(1)}, bf16[256,512]{1,0:T(8,128)(2,1)}, u32[]{:S(2)}) copy-start(bf16[256,512]{1,0:T(8,128)(2,1)} %get-tuple-element.10) | copy-start | bytes 786436
  99.1 1.9 %copy-start.3 = (f32[1024,1024]{1,0:T(8,128)}, f32[1024,1024]{1,0:T(8,128)S(1)}, u32[]{:S(2)}) copy-start(f32[1024,1024]{1,0:T(8,128)S(1)} %fusion.51) | copy-start | bytes 12582916
  110.1 30.0 %all-to-all-start.3 = ((bf16[2,32,32,256]{3,2,0,1:T(8,128)(2,1)}), bf16[2,32,32,256]{3,2,0,1:T(8,128)(2,1)}, u32[]{:S(2)}, u32[]{:S(2)}) async-start(bf16[2,32,32,256]{3,2,0,1:T(8,128)(2,1)} %copy.44), calls=%async_computation.3 | async-start | bytes 2097152 | tf_op jit(solution)/shard_map/all_to_all | solution.py:129
  114.8 8.0 %copy-start.12 = (pred[2048]{0:T(1024)(128)(4,1)}, pred[2048]{0:T(1024)(128)(4,1)S(1)}, u32[]{:S(2)}) copy-start(pred[2048]{0:T(1024)(128)(4,1)S(1)} %not_and_fusion) | copy-start | bytes 6148
where the time goes:
time: 167 us; the launch traced here: 166 us
  local copies, waits for them, and re-layouts  41.9 us (25%)
  matrix products  39.8 us (24%)
  waiting for transfers between devices  35.8 us (21%)
  other arithmetic  28.3 us (17%)
  starting transfers between devices  19.8 us (12%)
    all_to_all x1, waiting for transfers between devices, local(): lax.all_to_all(served, ('ev', 'node'), split_axis=1, concat_axis=1, tiled...  17 us
    dot_general x1, matrix products, local(): jnp.dot(write_mask, new_state, preferred_element_type=jnp.float32)  15.1 us
    all_to_all x1, waiting for transfers between devices, local(): lax.all_to_all(outgoing.reshape(2, devices_all, capacity, msg_width), ('e...  12.3 us
    gather x2, local copies, waits for them, and re-layouts, owner_lookup(): last_update[safe_rows]  11.9 us
    gather x1, local copies, waits for them, and re-layouts, local(): memory[safe_rows]  8.47 us
    dot_general x1, matrix products, gru_update(): jnp.dot(mean_msg, w_gru_in, preferred_element_type=jnp.float32) + b_gru_in  8.38 us
    gather x1, local copies, waits for them, and re-layouts, owner_lookup(): mem_rows = memory[safe_rows]  7.49 us
    all_to_all x1, starting transfers between devices, local(): lax.all_to_all(row_request.reshape(flat_shape), ('ev', 'node'), split_axi...  7.3 us
  transfers between devices with their start and end apart: 4, of which 3 were waited for; matrix products, arithmetic and copies ran while one was open for 29% of the time, Pallas kernels for 0%

commit v1 on v0

v1 whole, which is shorter than its diff:
```python
import functools

import jax
import jax.numpy as jnp
from jax import lax
from jax.experimental import pallas as pl
from jax.experimental.pallas import tpu as pltpu
from jax.sharding import PartitionSpec as P

MESH = pl.DeviceIdType.MESH
LANES = 128
F32 = jnp.float32
BF16 = jnp.bfloat16


def mm(a, b):
    return jnp.dot(a, b, preferred_element_type=F32)


def lanes_of(shape):
    return lax.broadcasted_iota(jnp.int32, shape, 1)


def subs_of(shape):
    return lax.broadcasted_iota(jnp.int32, shape, 0)


def exchange_kernel(
    n,
    per_row,
    slots,
    ints_ref,
    edge_ref,
    mem_ref,
    last_ref,
    freq_ref,
    phase_ref,
    win_ref,
    bmsg_ref,
    wout_ref,
    arrived_ref,
    rflat_ref,
    req_send,
    req_recv,
    rows_col,
    last_send,
    last_recv,
    row_send,
    row_recv,
    msg_send,
    msg_recv,
    msgs,
    send_sems,
    recv_sems,
):
    ev = lax.axis_index("ev")
    me = ev * per_row + lax.axis_index("node")
    events = edge_ref.shape[0]
    rows_count, width = mem_ref.shape
    hidden = wout_ref.shape[0]
    time_width = freq_ref.shape[1]
    cap = slots // 2
    rep = LANES // slots
    total = n * slots
    group = 256 // slots
    groups = n // group

    def coords(device):
        return (device // per_row, device % per_row)

    barrier = pltpu.get_barrier_semaphore()

    @pl.loop(1, n)
    def _(step):
        pl.semaphore_signal(
            barrier, inc=1, device_id=coords((me + step) % n), device_id_type=MESH
        )

    ints = ints_ref[...]
    padded = jnp.concatenate(
        [ints.astype(F32), jnp.zeros((LANES - 8, events), F32)], axis=0
    )
    cols = padded.T
    lane_e = lanes_of((events, LANES))
    sub_e = subs_of((LANES, events))
    tri_low = (lanes_of((events, events)) < subs_of((events, events))).astype(F32).astype(BF16)
    tri_up = (subs_of((events, events)) < lanes_of((events, events))).astype(F32).astype(BF16)

    hit_col, pos_col, slot_col, slot_row = [], [], [], []
    req_hi = jnp.zeros((LANES, LANES), F32)
    req_lo = jnp.zeros((LANES, LANES), F32)
    for side in range(2):
        owner_c = cols[:, side : side + 1].astype(jnp.int32)
        row_c = cols[:, 2 + side : 3 + side].astype(jnp.int32)
        hit_c = (owner_c == lane_e).astype(F32)
        hit_cb = hit_c.astype(BF16)
        pos_c = jnp.sum(mm(tri_low, hit_cb) * hit_c, axis=1, keepdims=True).astype(jnp.int32)
        pos_c = pos_c + side * cap
        owner_r = ints[side : side + 1, :]
        hit_r = (owner_r == sub_e).astype(F32)
        hit_rb = hit_r.astype(BF16)
        pos_r = jnp.sum(mm(hit_rb, tri_up) * hit_r, axis=0, keepdims=True).astype(jnp.int32)
        pos_r = pos_r + side * cap
        place = pos_c == lane_e % slots
        req_hi += mm(hit_rb, jnp.where(place, (row_c // 64 + 1).astype(F32), 0.0).astype(BF16))
        req_lo += mm(hit_rb, jnp.where(place, (row_c % 64).astype(F32), 0.0).astype(BF16))
        hit_col.append(hit_cb)
        pos_col.append(pos_c)
        slot_col.append(owner_c * slots + pos_c)
        slot_row.append(owner_r * slots + pos_r)
    request = jnp.where(req_hi > 0.5, (req_hi - 1.0) * 64.0 + req_lo, -1.0).astype(jnp.int32)
    for j in range(n):
        req_send[j] = request[j : j + 1, :]

    pl.semaphore_wait(barrier, n - 1)

    def send(phase, src, dst, device):
        return pltpu.make_async_remote_copy(
            src_ref=src,
            dst_ref=dst,
            send_sem=send_sems.at[phase],
            recv_sem=recv_sems.at[phase],
            device_id=coords(device),
            device_id_type=MESH,
        )

    def drain(sem, buf):
        part = buf.at[pl.ds(0, n - 1)]
        pltpu.make_async_copy(part, part, sem).wait()

    @pl.loop(1, n)
    def _(step):
        peer = (me + step) % n
        send(0, req_send.at[peer], req_recv.at[me], peer).start()

    req_recv[pl.ds(me, 1)] = req_send[pl.ds(me, 1)]
    drain(recv_sems.at[0], req_recv)

    lane_1 = lanes_of((1, LANES))
    blocks = []
    for b in range(n // rep):
        block = req_recv[b * rep]
        for q in range(1, rep):
            block = jnp.where(lane_1 // slots == q, req_recv[b * rep + q], block)
        blocks.append(block)
    flat = jnp.concatenate(blocks, axis=1)
    rflat_ref[...] = flat
    square = jnp.concatenate(
        [req_recv[j].astype(F32) for j in range(n)]
        + ([jnp.zeros((LANES - n, LANES), F32)] if n < LANES else []),
        axis=0,
    ).T.astype(jnp.int32)
    for j in range(n):
        rows_col[j * slots : (j + 1) * slots, :] = square[:slots, j : j + 1]

    @pl.loop(0, groups)
    def _(step):
        g = (ev * per_row // group + 1 + step) % groups
        wanted = rows_col[pl.ds(pl.multiple_of(g * 256, 256), 256), :]
        acc = jnp.zeros((256, width), F32)
        depth = 1024
        for k in range(rows_count // depth):
            onehot = (wanted == lanes_of((256, depth)) + k * depth).astype(F32).astype(BF16)
            acc += mm(onehot, mem_ref[k * depth : (k + 1) * depth, :])
        row_send[pl.ds(g * group, group)] = acc.astype(BF16).reshape(group, slots, width)
        for t in range(group):
            peer = g * group + t

            @pl.when(peer != me)
            def _():
                send(1, row_send.at[peer], row_recv.at[me], peer).start()

    last = last_ref[...]
    high_count = rows_count // LANES
    last_hi = (last // 64).astype(F32)
    last_lo = (last % 64).astype(F32)
    fill = jnp.zeros((LANES - high_count, LANES), F32)
    table_hi = jnp.concatenate([last_hi, fill], axis=0).T.astype(BF16)
    table_lo = jnp.concatenate([last_lo, fill], axis=0).T.astype(BF16)
    onehot_hi = (flat // LANES == subs_of((LANES, total))).astype(F32).astype(BF16)
    found = mm(table_hi, onehot_hi) * 64.0 + mm(table_lo, onehot_hi)
    kept = jnp.where(flat % LANES == subs_of((LANES, total)), found, 0.0)
    picked_last = jnp.sum(kept, axis=0, keepdims=True).astype(jnp.int32)
    for b in range(n // rep):
        last_send[b] = picked_last[:, b * LANES : (b + 1) * LANES]

    @pl.loop(1, n)
    def _(step):
        peer = (me + step) % n
        send(2, last_send.at[peer // rep], last_recv.at[me], peer).start()

    last_recv[pl.ds(me, 1)] = last_send[pl.ds(me // rep, 1)]
    row_recv[pl.ds(me, 1)] = row_send[pl.ds(me, 1)]

    edge_part = mm(edge_ref[...], win_ref[2 * width + time_width :, :]) + bmsg_ref[...]

    drain(recv_sems.at[2], last_recv)
    got = jnp.concatenate(
        [last_recv[j] for j in range(n)]
        + ([jnp.zeros((LANES - n, LANES), jnp.int32)] if n < LANES else []),
        axis=0,
    )
    got_hi = (got // 64).astype(F32).astype(BF16)
    got_lo = (got % 64).astype(F32).astype(BF16)
    moment = cols[:, 4:5]
    coded = []
    for side in range(2):
        spread = mm(hit_col[side], got_hi) * 64.0 + mm(hit_col[side], got_lo)
        here = pos_col[side] + (me % rep) * slots == lane_e
        before = jnp.sum(jnp.where(here, spread, 0.0), axis=1, keepdims=True)
        angle = (moment - before) * freq_ref[...] + phase_ref[...]
        coded.append(jnp.cos(angle).astype(BF16))

    drain(recv_sems.at[1], row_recv)
    fetched = row_recv[...].reshape(total, width)
    picked = []
    for side in range(2):
        pick = (slot_col[side] == lanes_of((events, total))).astype(F32).astype(BF16)
        picked.append(mm(pick, fetched).astype(BF16))
    for side in range(2):
        inputs = jnp.concatenate([picked[side], picked[1 - side], coded[side]], axis=1)
        hid = mm(inputs, win_ref[: 2 * width + time_width, :]) + edge_part
        hid = jnp.maximum(hid, 0.0).astype(BF16)
        msgs[side * events : (side + 1) * events, :] = mm(hid, wout_ref[...]).astype(BF16)

    slot_both = jnp.concatenate(slot_row, axis=1)

    @pl.loop(0, groups)
    def _(step):
        g = (ev * per_row // group + 1 + step) % groups
        placed = slot_both == subs_of((256, 2 * events)) + g * 256
        block = mm(placed.astype(F32).astype(BF16), msgs[...])
        msg_send[pl.ds(g * group, group)] = block.astype(BF16).reshape(group, slots, block.shape[1])
        for t in range(group):
            peer = g * group + t

            @pl.when(peer != me)
            def _():
                send(3, msg_send.at[peer], msg_recv.at[me], peer).start()

    msg_recv[pl.ds(me, 1)] = msg_send[pl.ds(me, 1)]
    drain(send_sems.at[0], req_send)
    drain(send_sems.at[1], row_send)
    drain(send_sems.at[2], last_recv)
    drain(recv_sems.at[3], msg_recv)
    arrived_ref[...] = msg_recv[...].reshape(arrived_ref.shape)
    drain(send_sems.at[3], msg_send)


def update_kernel(rflat_ref, msg_ref, mem_ref, win_ref, bin_ref, whid_ref, out_ref):
    rows, width = mem_ref.shape
    total = msg_ref.shape[0]
    base = pl.program_id(0) * rows
    hits = (rflat_ref[...] == subs_of((rows, total)) + base).astype(F32)
    count = jnp.sum(hits, axis=1, keepdims=True)
    summed = mm(hits.astype(BF16), msg_ref[...])
    mean = (summed / jnp.maximum(count, 1.0)).astype(BF16)
    state = mem_ref[...]
    gi = mm(mean, win_ref[...]) + bin_ref[...]
    gh = mm(state, whid_ref[...])
    reset = jax.nn.sigmoid(gi[:, :width] + gh[:, :width])
    update = jax.nn.sigmoid(gi[:, width : 2 * width] + gh[:, width : 2 * width])
    candid = jnp.tanh(gi[:, 2 * width :] + reset * gh[:, 2 * width :])
    fresh = (1.0 - update) * candid + update * state.astype(F32)
    out_ref[...] = jnp.where(count > 0.5, fresh, state.astype(F32)).astype(BF16)


def local(
    per_row,
    src_owner,
    src_row,
    dst_owner,
    dst_row,
    event_time,
    edge_feat,
    memory,
    last_update,
    time_freq,
    time_phase,
    w_msg_in,
    b_msg,
    w_msg_out,
    w_gru_in,
    b_gru_in,
    w_gru_hid,
):
    n = lax.axis_size(("ev", "node"))
    events = edge_feat.shape[0]
    slots = 2 * max(2, 2 * events // n)
    rows_count, width = memory.shape
    msg_width = w_msg_out.shape[1]
    total = n * slots
    zero = jnp.zeros_like(src_row)
    ints = jnp.stack(
        [src_owner[:, 0], dst_owner[:, 0], src_row, dst_row, event_time, zero, zero, zero]
    )
    vmem = pl.BlockSpec(memory_space=pltpu.VMEM)
    arrived, rflat = pl.pallas_call(
        functools.partial(exchange_kernel, n, per_row, slots),
        out_shape=(
            jax.ShapeDtypeStruct((total, msg_width), BF16),
            jax.ShapeDtypeStruct((1, total), jnp.int32),
        ),
        in_specs=[vmem] * 9,
        out_specs=(vmem, vmem),
        scratch_shapes=[
            pltpu.VMEM((n, 1, LANES), jnp.int32),
            pltpu.VMEM((n, 1, LANES), jnp.int32),
            pltpu.VMEM((total, 1), jnp.int32),
            pltpu.VMEM((n * slots // LANES, 1, LANES), jnp.int32),
            pltpu.VMEM((n, 1, LANES), jnp.int32),
            pltpu.VMEM((n, slots, width), BF16),
            pltpu.VMEM((n, slots, width), BF16),
            pltpu.VMEM((n, slots, msg_width), BF16),
            pltpu.VMEM((n, slots, msg_width), BF16),
            pltpu.VMEM((2 * events, msg_width), BF16),
            pltpu.SemaphoreType.DMA((4,)),
            pltpu.SemaphoreType.DMA((4,)),
        ],
        compiler_params=pltpu.CompilerParams(
            collective_id=0, has_side_effects=True, vmem_limit_bytes=48 * 1024 * 1024
        ),
        name="exchange",
    )(
        ints,
        edge_feat,
        memory,
        last_update.reshape(rows_count // LANES, LANES),
        time_freq[None, :],
        time_phase[None, :],
        w_msg_in,
        b_msg[None, :],
        w_msg_out,
    )
    chunk = min(512, rows_count)

    def fixed(*shape):
        return pl.BlockSpec(shape, lambda i: (0, 0))

    return pl.pallas_call(
        update_kernel,
        grid=(rows_count // chunk,),
        out_shape=jax.ShapeDtypeStruct(memory.shape, BF16),
        in_specs=[
            fixed(1, total),
            fixed(total, msg_width),
            pl.BlockSpec((chunk, width), lambda i: (i, 0)),
            fixed(*w_gru_in.shape),
            fixed(1, b_gru_in.shape[0]),
            fixed(*w_gru_hid.shape),
        ],
        out_specs=pl.BlockSpec((chunk, width), lambda i: (i, 0)),
        compiler_params=pltpu.CompilerParams(vmem_limit_bytes=48 * 1024 * 1024),
        name="update",
    )(rflat, arrived, memory, w_gru_in, b_gru_in[None, :], w_gru_hid)


def solution(mesh):
    in_specs = (
        P(("ev", "node"), None),
        P(("ev", "node")),
        P(("ev", "node"), None),
        P(("ev", "node")),
        P(("ev", "node")),
        P(("ev", "node"), None),
        P(("ev", "node"), None),
        P(("ev", "node")),
        P(),
        P(),
        P(),
        P(),
        P(),
        P(),
        P(),
        P(),
    )
    out_specs = P(("ev", "node"), None)
    return jax.shard_map(
        functools.partial(local, mesh.shape["node"]),
        mesh=mesh,
        in_specs=in_specs,
        out_specs=out_specs,
        check_vma=False,
    )
```

time: 167 us -> 93.2 us (0.56)
  the two profiles are of different devices: /device:TPU:0 before, /device:TPU:31 now
where the time goes in v1:
time: 93.2 us; the launch traced here: 92.8 us
  Pallas kernels  83.9 us (90%)
  local copies, waits for them, and re-layouts  8.85 us (9%)
    pallas_call x1, Pallas kernels, local(): pl.pallas_call(functools.partial(exchange_kernel, n, per_row, slots), out...  66 us
    pallas_call x1, Pallas kernels, local(): pl.pallas_call(update_kernel, grid=(rows_count // chunk,), out_shape=jax....  17.8 us
    unnamed x22, local copies, waits for them, and re-layouts  7.38 us

profile of v1, /device:TPU:31, one launch (start us, length us, event | category | flops | bytes accessed | tf_op | source)
XLA Modules:
  0.0 92.8 jit_solution(10521650725602003059)
XLA Ops:
  0.0 0.7 broadcast_in_dim.15.bin_ref
  0.7 0.8 stack.19.ints_ref
  1.5 0.0 copy-start
  1.5 1.6 %copy-done = bf16[4096,256]{1,0:T(8,128)(2,1)S(1)} copy-done((bf16[4096,256]{1,0:T(8,128)(2,1)S(1)}, bf16[4096,256]{1,0:T(8,128)(2,1)}, u32[]{:S(2)}) %copy-start) | copy-done | bytes 2097176
  3.1 0.0 copy-start.2
  3.1 1.2 %copy-done.2 = bf16[896,512]{1,0:T(8,128)(2,1)S(1)} copy-done((bf16[896,512]{1,0:T(8,128)(2,1)S(1)}, bf16[896,512]{1,0:T(8,128)(2,1)}, u32[]{:S(2)}) %copy-start.2) | copy-done | bytes 917528
  4.2 0.0 copy-start.5
  4.2 0.9 %copy-done.5 = bf16[512,256]{1,0:T(8,128)(2,1)S(1)} copy-done((bf16[512,256]{1,0:T(8,128)(2,1)S(1)}, bf16[512,256]{1,0:T(8,128)(2,1)}, u32[]{:S(2)}) %copy-start.5) | copy-done | bytes 262168
  5.2 0.0 copy-start.6
  5.2 0.9 %copy-done.6 = bf16[512,256]{1,0:T(8,128)(2,1)S(1)} copy-done((bf16[512,256]{1,0:T(8,128)(2,1)S(1)}, bf16[512,256]{1,0:T(8,128)(2,1)}, u32[]{:S(2)}) %copy-start.6) | copy-done | bytes 262168
  6.1 0.0 copy-start.7
  6.1 0.7 copy-done.7
  6.9 0.0 copy-start.8
  6.9 0.7 copy-done.8
  7.5 0.0 copy-start.9
  7.5 0.7 copy-done.9
  8.2 0.0 copy-start.10
  8.2 0.7 copy-done.10
  8.9 0.0 copy-start.1
  8.9 66.0 %exchange.1 = (bf16[2048,256]{1,0:T(8,128)(2,1)S(1)}, s32[1,2048]{1,0:T(1,128)S(1)}) custom-call(s32[8,512]{1,0:T(8,128)S(1)} %stack.19.ints_ref, bf16[512,256]{1,0:T(8,128)(2,1)S(1)} %copy-done.5, bf16[4096,256]{1,0:T(8,128)(2,1)S(1)} %copy-done, s32[32,128]{1,0:T(8,128)S(1)} %bitcast.9, f32[1,128]{1,0:T(1,128)S(1)} %bitcast.11, f32[1,128]{1,0:T(1,128)S(1)} %bitcast.12, ...), custom_call_target="tpu_custom_call" | custom-call | tf_op jit(solution)/shard_map/exchange/pallas_call | solution.py:298
  74.9 0.0 copy-done.1
  74.9 0.0 copy-done.3
  74.9 0.0 copy-done.4
  74.9 17.8 %update.1 = bf16[4096,256]{1,0:T(8,128)(2,1)} custom-call(s32[1,2048]{1,0:T(1,128)S(1)} %get-tuple-element.7.rflat_ref, bf16[2048,256]{1,0:T(8,128)(2,1)S(1)} %get-tuple-element.8.msg_ref, bf16[4096,256]{1,0:T(8,128)(2,1)S(1)} %copy-done.1, bf16[256,768]{1,0:T(8,128)(2,1)S(1)} %copy-done.3, f32[1,768]{1,0:T(1,128)S(1)} %broadcast_in_dim.15.bin_ref, ...), custom_call_target="tpu_custom_call" | custom-call | tf_op jit(solution)/shard_map/update/pallas_call | solution.py:340
  (4 shorter events, 0.0 us)
Async XLA Ops:
  1.5 1.6 %copy-start = (bf16[4096,256]{1,0:T(8,128)(2,1)S(1)}, bf16[4096,256]{1,0:T(8,128)(2,1)}, u32[]{:S(2)}) copy-start(bf16[4096,256]{1,0:T(8,128)(2,1)} %mem_ref.3) | copy-start | bytes 6291460
  3.1 1.2 %copy-start.2 = (bf16[896,512]{1,0:T(8,128)(2,1)S(1)}, bf16[896,512]{1,0:T(8,128)(2,1)}, u32[]{:S(2)}) copy-start(bf16[896,512]{1,0:T(8,128)(2,1)} %win_ref.2) | copy-start | bytes 2752516
  4.2 0.9 %copy-start.5 = (bf16[512,256]{1,0:T(8,128)(2,1)S(1)}, bf16[512,256]{1,0:T(8,128)(2,1)}, u32[]{:S(2)}) copy-start(bf16[512,256]{1,0:T(8,128)(2,1)} %edge_ref.1) | copy-start | bytes 786436
  5.2 0.9 %copy-start.6 = (bf16[512,256]{1,0:T(8,128)(2,1)S(1)}, bf16[512,256]{1,0:T(8,128)(2,1)}, u32[]{:S(2)}) copy-start(bf16[512,256]{1,0:T(8,128)(2,1)} %wout_ref.1) | copy-start | bytes 786436
  6.1 0.7 copy-start.7
  6.9 0.7 copy-start.8
  7.5 0.7 copy-start.9
  8.2 0.7 copy-start.10
  8.9 66.1 %copy-start.1 = (bf16[4096,256]{1,0:T(8,128)(2,1)S(1)}, bf16[4096,256]{1,0:T(8,128)(2,1)}, u32[]{:S(2)}) copy-start(bf16[4096,256]{1,0:T(8,128)(2,1)} %mem_ref.3) | copy-start | bytes 6291460
  8.9 66.1 %copy-start.3 = (bf16[256,768]{1,0:T(8,128)(2,1)S(1)}, bf16[256,768]{1,0:T(8,128)(2,1)}, u32[]{:S(2)}) copy-start(bf16[256,768]{1,0:T(8,128)(2,1)} %win_ref.3) | copy-start | bytes 1179652
  8.9 66.1 %copy-start.4 = (bf16[256,768]{1,0:T(8,128)(2,1)S(1)}, bf16[256,768]{1,0:T(8,128)(2,1)}, u32[]{:S(2)}) copy-start(bf16[256,768]{1,0:T(8,128)(2,1)} %whid_ref.1) | copy-start | bytes 1179652

commit v2 on v1

--- a/solution.py
+++ b/solution.py
@@ -29,17 +29,26 @@
     n,
     per_row,
     slots,
-    ints_ref,
+    events,
+    time_width,
+    params_hbm,
+    last_hbm,
+    mem_hbm,
+    edge_hbm,
+    win_hbm,
+    wout_hbm,
+    gin_hbm,
+    ghid_hbm,
+    out_hbm,
+    params_ref,
+    last_ref,
+    mem_ref,
     edge_ref,
-    mem_ref,
-    last_ref,
-    freq_ref,
-    phase_ref,
     win_ref,
-    bmsg_ref,
     wout_ref,
-    arrived_ref,
-    rflat_ref,
+    gin_ref,
+    ghid_ref,
+    out_ref,
     req_send,
     req_recv,
     rows_col,
@@ -50,15 +59,20 @@
     msg_send,
     msg_recv,
     msgs,
+    flat_ref,
+    hits_ref,
+    count_ref,
+    state_ref,
+    sum_ref,
     send_sems,
     recv_sems,
+    load_sems,
+    store_sem,
 ):
     ev = lax.axis_index("ev")
     me = ev * per_row + lax.axis_index("node")
-    events = edge_ref.shape[0]
     rows_count, width = mem_ref.shape
     hidden = wout_ref.shape[0]
-    time_width = freq_ref.shape[1]
     cap = slots // 2
     rep = LANES // slots
     total = n * slots
@@ -76,10 +90,32 @@
             barrier, inc=1, device_id=coords((me + step) % n), device_id_type=MESH
         )
 
-    ints = ints_ref[...]
+    loads = [
+        pltpu.make_async_copy(src, dst, load_sems.at[k])
+        for k, (src, dst) in enumerate(
+            [
+                (params_hbm, params_ref),
+                (last_hbm, last_ref),
+                (mem_hbm, mem_ref),
+                (edge_hbm, edge_ref),
+                (win_hbm, win_ref),
+                (wout_hbm, wout_ref),
+                (ghid_hbm, ghid_ref),
+                (gin_hbm, gin_ref),
+            ]
+        )
+    ]
+    for load in loads:
+        load.start()
+    loads[0].wait()
+    params = params_ref[...]
+    ints = params[:, :events].astype(jnp.int32)
     padded = jnp.concatenate(
-        [ints.astype(F32), jnp.zeros((LANES - 8, events), F32)], axis=0
+        [params[:, :events], jnp.zeros((LANES - 8, events), F32)], axis=0
     )
+    freq = params[7:8, :time_width]
+    phase = params[7:8, time_width : 2 * time_width]
+    gate = params[6:7, : 3 * width]
     cols = padded.T
     lane_e = lanes_of((events, LANES))
     sub_e = subs_of((LANES, events))
@@ -144,7 +180,8 @@
             block = jnp.where(lane_1 // slots == q, req_recv[b * rep + q], block)
         blocks.append(block)
     flat = jnp.concatenate(blocks, axis=1)
-    rflat_ref[...] = flat
+    for g in range(groups):
+        flat_ref[g] = flat[:, g * 256 : (g + 1) * 256]
     square = jnp.concatenate(
         [req_recv[j].astype(F32) for j in range(n)]
         + ([jnp.zeros((LANES - n, LANES), F32)] if n < LANES else []),
@@ -153,9 +190,11 @@
     for j in range(n):
         rows_col[j * slots : (j + 1) * slots, :] = square[:slots, j : j + 1]
 
+    loads[2].wait()
+
     @pl.loop(0, groups)
     def _(step):
-        g = (ev * per_row // group + 1 + step) % groups
+        g = (me // group + 1 + step) % groups
         wanted = rows_col[pl.ds(pl.multiple_of(g * 256, 256), 256), :]
         acc = jnp.zeros((256, width), F32)
         depth = 1024
@@ -164,12 +203,13 @@
             acc += mm(onehot, mem_ref[k * depth : (k + 1) * depth, :])
         row_send[pl.ds(g * group, group)] = acc.astype(BF16).reshape(group, slots, width)
         for t in range(group):
-            peer = g * group + t
+            peer = g * group + (me + t) % group
 
             @pl.when(peer != me)
             def _():
                 send(1, row_send.at[peer], row_recv.at[me], peer).start()
 
+    loads[1].wait()
     last = last_ref[...]
     high_count = rows_count // LANES
     last_hi = (last // 64).astype(F32)
@@ -192,7 +232,22 @@
     last_recv[pl.ds(me, 1)] = last_send[pl.ds(me // rep, 1)]
     row_recv[pl.ds(me, 1)] = row_send[pl.ds(me, 1)]
 
-    edge_part = mm(edge_ref[...], win_ref[2 * width + time_width :, :]) + bmsg_ref[...]
+    for load in loads[3:]:
+        load.wait()
+    edge_part = mm(edge_ref[...], win_ref[2 * width + time_width :, :]) + params[5:6, :hidden]
+    chunk = 512
+
+    @pl.loop(0, rows_count // chunk)
+    def _(step):
+        base = pl.multiple_of(step * chunk, chunk)
+        count = jnp.zeros((chunk, 1), F32)
+        for g in range(groups):
+            hits = (flat_ref[g] == subs_of((chunk, 256)) + base).astype(F32)
+            hits_ref[g, pl.ds(base, chunk), :] = hits.astype(BF16)
+            count += jnp.sum(hits, axis=1, keepdims=True)
+        count_ref[pl.ds(base, chunk), :] = count
+        state_ref[pl.ds(base, chunk), :] = mm(mem_ref[pl.ds(base, chunk), :], ghid_ref[...])
+
 
     drain(recv_sems.at[2], last_recv)
     got = jnp.concatenate(
@@ -208,7 +263,7 @@
         spread = mm(hit_col[side], got_hi) * 64.0 + mm(hit_col[side], got_lo)
         here = pos_col[side] + (me % rep) * slots == lane_e
         before = jnp.sum(jnp.where(here, spread, 0.0), axis=1, keepdims=True)
-        angle = (moment - before) * freq_ref[...] + phase_ref[...]
+        angle = (moment - before) * freq + phase
         coded.append(jnp.cos(angle).astype(BF16))
 
     drain(recv_sems.at[1], row_recv)
@@ -225,44 +280,72 @@
 
     slot_both = jnp.concatenate(slot_row, axis=1)
 
-    @pl.loop(0, groups)
-    def _(step):
-        g = (ev * per_row // group + 1 + step) % groups
-        placed = slot_both == subs_of((256, 2 * events)) + g * 256
-        block = mm(placed.astype(F32).astype(BF16), msgs[...])
-        msg_send[pl.ds(g * group, group)] = block.astype(BF16).reshape(group, slots, block.shape[1])
-        for t in range(group):
-            peer = g * group + t
-
-            @pl.when(peer != me)
-            def _():
-                send(3, msg_send.at[peer], msg_recv.at[me], peer).start()
-
+    half = groups // 2
+
+    def push(first, stop, kind):
+        @pl.loop(first, stop)
+        def _(step):
+            g = (me // group + 1 + step) % groups
+            placed = slot_both == subs_of((256, 2 * events)) + g * 256
+            block = mm(placed.astype(F32).astype(BF16), msgs[...])
+            msg_send[pl.ds(g * group, group)] = block.astype(BF16).reshape(
+                group, slots, block.shape[1]
+            )
+            for t in range(group):
+                peer = g * group + (me + t) % group
+
+                @pl.when(peer != me)
+                def _():
+                    send(kind, msg_send.at[peer], msg_recv.at[me], peer).start()
+
+    push(0, half, 3)
+    push(half, groups, 4)
     msg_recv[pl.ds(me, 1)] = msg_send[pl.ds(me, 1)]
     drain(send_sems.at[0], req_send)
     drain(send_sems.at[1], row_send)
     drain(send_sems.at[2], last_recv)
-    drain(recv_sems.at[3], msg_recv)
-    arrived_ref[...] = msg_recv[...].reshape(arrived_ref.shape)
-    drain(send_sems.at[3], msg_send)
-
-
-def update_kernel(rflat_ref, msg_ref, mem_ref, win_ref, bin_ref, whid_ref, out_ref):
-    rows, width = mem_ref.shape
-    total = msg_ref.shape[0]
-    base = pl.program_id(0) * rows
-    hits = (rflat_ref[...] == subs_of((rows, total)) + base).astype(F32)
-    count = jnp.sum(hits, axis=1, keepdims=True)
-    summed = mm(hits.astype(BF16), msg_ref[...])
-    mean = (summed / jnp.maximum(count, 1.0)).astype(BF16)
-    state = mem_ref[...]
-    gi = mm(mean, win_ref[...]) + bin_ref[...]
-    gh = mm(state, whid_ref[...])
-    reset = jax.nn.sigmoid(gi[:, :width] + gh[:, :width])
-    update = jax.nn.sigmoid(gi[:, width : 2 * width] + gh[:, width : 2 * width])
-    candid = jnp.tanh(gi[:, 2 * width :] + reset * gh[:, 2 * width :])
-    fresh = (1.0 - update) * candid + update * state.astype(F32)
-    out_ref[...] = jnp.where(count > 0.5, fresh, state.astype(F32)).astype(BF16)
+
+    def settle(sem, buf, blocks_moved):
+        part = buf.at[pl.ds(0, blocks_moved)]
+        pltpu.make_async_copy(part, part, sem).wait()
+
+    def gathered(base, steps):
+        acc = jnp.zeros((chunk, msgs.shape[1]), F32)
+        for step in steps:
+            g = (me // group + groups - 1 - step) % groups
+            block = msg_recv[pl.ds(g * group, group)].reshape(256, msgs.shape[1])
+            acc += mm(hits_ref[g, pl.ds(base, chunk), :], block)
+        return acc
+
+    settle(recv_sems.at[3], msg_recv, half * group)
+
+    @pl.loop(0, rows_count // chunk)
+    def _(step):
+        base = pl.multiple_of(step * chunk, chunk)
+        sum_ref[pl.ds(base, chunk), :] = gathered(base, range(half))
+
+    settle(recv_sems.at[4], msg_recv, half * group - 1)
+
+    @pl.loop(0, rows_count // chunk)
+    def _(step):
+        base = pl.multiple_of(step * chunk, chunk)
+        rows = pl.ds(base, chunk)
+        count = count_ref[rows, :]
+        summed = sum_ref[rows, :] + gathered(base, range(half, groups))
+        mean = (summed / jnp.maximum(count, 1.0)).astype(BF16)
+        state = mem_ref[rows, :].astype(F32)
+        gi = mm(mean, gin_ref[...]) + gate
+        gh = state_ref[rows, :]
+        reset = 0.5 * jnp.tanh(0.5 * (gi[:, :width] + gh[:, :width])) + 0.5
+        update = 0.5 * jnp.tanh(0.5 * (gi[:, width : 2 * width] + gh[:, width : 2 * width])) + 0.5
+        candid = jnp.tanh(gi[:, 2 * width :] + reset * gh[:, 2 * width :])
+        fresh = candid + update * (state - candid)
+        out_ref[rows, :] = jnp.where(count > 0.5, fresh, state).astype(BF16)
+        pltpu.make_async_copy(out_ref.at[rows], out_hbm.at[rows], store_sem).start()
+
+    settle(send_sems.at[3], msg_send, half * group)
+    settle(send_sems.at[4], msg_send, half * group - 1)
+    pltpu.make_async_copy(out_ref, out_hbm, store_sem).wait()
 
 
 def local(
@@ -290,20 +373,37 @@
     rows_count, width = memory.shape
     msg_width = w_msg_out.shape[1]
     total = n * slots
-    zero = jnp.zeros_like(src_row)
-    ints = jnp.stack(
-        [src_owner[:, 0], dst_owner[:, 0], src_row, dst_row, event_time, zero, zero, zero]
+    span = max(events, 3 * width, w_msg_out.shape[0], 2 * time_freq.shape[0])
+    small = [
+        src_owner[:, 0],
+        dst_owner[:, 0],
+        src_row,
+        dst_row,
+        event_time,
+        b_msg,
+        b_gru_in,
+        jnp.concatenate([time_freq, time_phase]),
+    ]
+    params = jnp.stack([jnp.pad(x.astype(F32), (0, span - x.shape[0])) for x in small])
+    operands = (
+        params,
+        last_update.reshape(rows_count // LANES, LANES),
+        memory,
+        edge_feat,
+        w_msg_in,
+        w_msg_out,
+        w_gru_in,
+        w_gru_hid,
     )
-    vmem = pl.BlockSpec(memory_space=pltpu.VMEM)
-    arrived, rflat = pl.pallas_call(
-        functools.partial(exchange_kernel, n, per_row, slots),
-        out_shape=(
-            jax.ShapeDtypeStruct((total, msg_width), BF16),
-            jax.ShapeDtypeStruct((1, total), jnp.int32),
-        ),
-        in_specs=[vmem] * 9,
-        out_specs=(vmem, vmem),
-        scratch_shapes=[
+    anywhere = pl.BlockSpec(memory_space=pl.ANY)
+    return pl.pallas_call(
+        functools.partial(exchange_kernel, n, per_row, slots, events, time_freq.shape[0]),
+        out_shape=jax.ShapeDtypeStruct(memory.shape, BF16),
+        in_specs=[anywhere] * len(operands),
+        out_specs=anywhere,
+        scratch_shapes=[pltpu.VMEM(x.shape, x.dtype) for x in operands]
+        + [
+            pltpu.VMEM(memory.shape, BF16),
             pltpu.VMEM((n, 1, LANES), jnp.int32),
             pltpu.VMEM((n, 1, LANES), jnp.int32),
             pltpu.VMEM((total, 1), jnp.int32),
@@ -314,45 +414,21 @@
             pltpu.VMEM((n, slots, msg_width), BF16),
             pltpu.VMEM((n, slots, msg_width), BF16),
             pltpu.VMEM((2 * events, msg_width), BF16),
-            pltpu.SemaphoreType.DMA((4,)),
-            pltpu.SemaphoreType.DMA((4,)),
+            pltpu.VMEM((total // 256, 1, 256), jnp.int32),
+            pltpu.VMEM((total // 256, rows_count, 256), BF16),
+            pltpu.VMEM((rows_count, 1), F32),
+            pltpu.VMEM((rows_count, 3 * width), F32),
+            pltpu.VMEM((rows_count, msg_width), F32),
+            pltpu.SemaphoreType.DMA((5,)),
+            pltpu.SemaphoreType.DMA((5,)),
+            pltpu.SemaphoreType.DMA((len(operands),)),
+            pltpu.SemaphoreType.DMA,
         ],
         compiler_params=pltpu.CompilerParams(
-            collective_id=0, has_side_effects=True, vmem_limit_bytes=48 * 1024 * 1024
+            collective_id=0, has_side_effects=True, vmem_limit_bytes=58 * 1024 * 1024
         ),
         name="exchange",
-    )(
-        ints,
-        edge_feat,
-        memory,
-        last_update.reshape(rows_count // LANES, LANES),
-        time_freq[None, :],
-        time_phase[None, :],
-        w_msg_in,
-        b_msg[None, :],
-        w_msg_out,
-    )
-    chunk = min(512, rows_count)
-
-    def fixed(*shape):
-        return pl.BlockSpec(shape, lambda i: (0, 0))
-
-    return pl.pallas_call(
-        update_kernel,
-        grid=(rows_count // chunk,),
-        out_shape=jax.ShapeDtypeStruct(memory.shape, BF16),
-        in_specs=[
-            fixed(1, total),
-            fixed(total, msg_width),
-            pl.BlockSpec((chunk, width), lambda i: (i, 0)),
-            fixed(*w_gru_in.shape),
-            fixed(1, b_gru_in.shape[0]),
-            fixed(*w_gru_hid.shape),
-        ],
-        out_specs=pl.BlockSpec((chunk, width), lambda i: (i, 0)),
-        compiler_params=pltpu.CompilerParams(vmem_limit_bytes=48 * 1024 * 1024),
-        name="update",
-    )(rflat, arrived, memory, w_gru_in, b_gru_in[None, :], w_gru_hid)
+    )(*operands)
 
 
 def solution(mesh):

time: 93.2 us -> 88.1 us (0.945)
  Pallas kernels: 83.9 us -> 78.5 us
  other arithmetic: 0 us -> 4.1 us
  local copies, waits for them, and re-layouts: 8.85 us -> 5.14 us
    pallas_call x2 -> x1, Pallas kernels: 83.9 us -> 78.5 us  [local(): pl.pallas_call(functools.partial(exchange_kernel, n, per_row, slots, even...]
    unnamed x22 -> x1, local copies, waits for them, and re-layouts: 7.38 us -> 3.05 us
    convert_element_type x0 -> x5, other arithmetic: none -> 3.42 us  [local(): x.astype(F32)]
where the time goes in v2:
time: 88.1 us; the launch traced here: 87.8 us
  Pallas kernels  78.5 us (89%)
  local copies, waits for them, and re-layouts  5.14 us (6%)
  other arithmetic  4.1 us (5%)
    pallas_call x1, Pallas kernels, local(): pl.pallas_call(functools.partial(exchange_kernel, n, per_row, slots, even...  78.5 us
    convert_element_type x5, other arithmetic, local(): x.astype(F32)  3.42 us
    unnamed x1, local copies, waits for them, and re-layouts  3.05 us

profile of v2, /device:TPU:31, one launch (start us, length us, event | category | flops | bytes accessed | tf_op | source)
XLA Modules:
  0.0 87.8 jit_solution(16798948680516822390)
XLA Ops:
  0.0 0.7 convert_element_type.30
  0.7 0.7 convert_element_type.34
  1.4 0.7 convert_element_type.32
  2.1 0.7 convert_element_type.35
  2.8 0.7 convert_element_type.36
  3.5 0.7 stack.33
  4.2 0.7 select_maximum_fusion
  4.9 0.7 pad.28
  5.6 0.6 stack.35.params_hbm
  6.2 78.5 %exchange.1 = bf16[4096,256]{1,0:T(8,128)(2,1)} custom-call(f32[8,768]{1,0:T(8,128)} %stack.35.params_hbm, s32[32,128]{1,0:T(8,128)} %bitcast.3, bf16[4096,256]{1,0:T(8,128)(2,1)} %mem_hbm.1, bf16[512,256]{1,0:T(8,128)(2,1)} %edge_hbm.1, bf16[896,512]{1,0:T(8,128)(2,1)} %win_hbm.1, bf16[512,256]{1,0:T(8,128)(2,1)} %wout_hbm.1, bf16[256,768]{1,0:T(8,128)(2,1)} %gin_hbm.1, ...), custom_call_target="tpu_custom_call" | custom-call | tf_op jit(solution)/shard_map/exchange/pallas_call | solution.py:399
  84.8 3.0 %copy.18 = bf16[4096,256]{1,0:T(8,128)(2,1)} copy(bf16[4096,256]{1,0:T(8,128)(2,1)} %exchange.1) | data formatting | bytes 4194304
  (12 shorter events, 0.1 us)

commit v3 on v2

--- a/solution.py
+++ b/solution.py
@@ -31,7 +31,15 @@
     slots,
     events,
     time_width,
-    params_hbm,
+    so_hbm,
+    do_hbm,
+    sr_hbm,
+    dr_hbm,
+    et_hbm,
+    freq_hbm,
+    phase_hbm,
+    bmsg_hbm,
+    bgru_hbm,
     last_hbm,
     mem_hbm,
     edge_hbm,
@@ -40,7 +48,15 @@
     gin_hbm,
     ghid_hbm,
     out_hbm,
-    params_ref,
+    so_ref,
+    do_ref,
+    sr_ref,
+    dr_ref,
+    et_ref,
+    freq_ref,
+    phase_ref,
+    bmsg_ref,
+    bgru_ref,
     last_ref,
     mem_ref,
     edge_ref,
@@ -52,6 +68,8 @@
     req_send,
     req_recv,
     rows_col,
+    pick_ref,
+    place_ref,
     last_send,
     last_recv,
     row_send,
@@ -82,6 +100,15 @@
     def coords(device):
         return (device // per_row, device % per_row)
 
+    def mirrored(step):
+        k = (step + groups // 2) % groups
+        k = k + (step // (groups // 2)) * (groups // 2 - 1 - 2 * k)
+        g, unit = 0, 1
+        while unit < groups:
+            g = g + unit * ((me // group // unit + k // unit) % 2)
+            unit = 2 * unit
+        return g
+
     barrier = pltpu.get_barrier_semaphore()
 
     @pl.loop(1, n)
@@ -94,8 +121,16 @@
         pltpu.make_async_copy(src, dst, load_sems.at[k])
         for k, (src, dst) in enumerate(
             [
-                (params_hbm, params_ref),
+                (so_hbm, so_ref),
+                (do_hbm, do_ref),
+                (sr_hbm, sr_ref),
+                (dr_hbm, dr_ref),
+                (et_hbm, et_ref),
                 (last_hbm, last_ref),
+                (freq_hbm, freq_ref),
+                (phase_hbm, phase_ref),
+                (bmsg_hbm, bmsg_ref),
+                (bgru_hbm, bgru_ref),
                 (mem_hbm, mem_ref),
                 (edge_hbm, edge_ref),
                 (win_hbm, win_ref),
@@ -107,15 +142,16 @@
     ]
     for load in loads:
         load.start()
-    loads[0].wait()
-    params = params_ref[...]
-    ints = params[:, :events].astype(jnp.int32)
+    for load in loads[:5]:
+        load.wait()
+    ints = jnp.concatenate(
+        [so_ref[...], do_ref[...], sr_ref[...], dr_ref[...], et_ref[...]]
+        + [jnp.zeros((3, events), jnp.int32)],
+        axis=0,
+    )
     padded = jnp.concatenate(
-        [params[:, :events], jnp.zeros((LANES - 8, events), F32)], axis=0
+        [ints.astype(F32), jnp.zeros((LANES - 8, events), F32)], axis=0
     )
-    freq = params[7:8, :time_width]
-    phase = params[7:8, time_width : 2 * time_width]
-    gate = params[6:7, : 3 * width]
     cols = padded.T
     lane_e = lanes_of((events, LANES))
     sub_e = subs_of((LANES, events))
@@ -169,6 +205,11 @@
         peer = (me + step) % n
         send(0, req_send.at[peer], req_recv.at[me], peer).start()
 
+    for side in range(2):
+        for g in range(groups):
+            near = slot_col[side] == lanes_of((events, 256)) + g * 256
+            pick_ref[side, :, g * 256 : (g + 1) * 256] = near.astype(F32).astype(BF16)
+
     req_recv[pl.ds(me, 1)] = req_send[pl.ds(me, 1)]
     drain(recv_sems.at[0], req_recv)
 
@@ -190,11 +231,11 @@
     for j in range(n):
         rows_col[j * slots : (j + 1) * slots, :] = square[:slots, j : j + 1]
 
-    loads[2].wait()
-
-    @pl.loop(0, groups)
-    def _(step):
-        g = (me // group + 1 + step) % groups
+    for load in loads[5:]:
+        load.wait()
+
+    def serve(step):
+        g = mirrored(step)
         wanted = rows_col[pl.ds(pl.multiple_of(g * 256, 256), 256), :]
         acc = jnp.zeros((256, width), F32)
         depth = 1024
@@ -209,7 +250,7 @@
             def _():
                 send(1, row_send.at[peer], row_recv.at[me], peer).start()
 
-    loads[1].wait()
+    serve(0)
     last = last_ref[...]
     high_count = rows_count // LANES
     last_hi = (last // 64).astype(F32)
@@ -229,25 +270,31 @@
         peer = (me + step) % n
         send(2, last_send.at[peer // rep], last_recv.at[me], peer).start()
 
+    pl.loop(1, groups)(serve)
     last_recv[pl.ds(me, 1)] = last_send[pl.ds(me // rep, 1)]
     row_recv[pl.ds(me, 1)] = row_send[pl.ds(me, 1)]
 
-    for load in loads[3:]:
-        load.wait()
-    edge_part = mm(edge_ref[...], win_ref[2 * width + time_width :, :]) + params[5:6, :hidden]
+    edge_part = mm(edge_ref[...], win_ref[2 * width + time_width :, :]) + bmsg_ref[...]
     chunk = 512
 
     @pl.loop(0, rows_count // chunk)
     def _(step):
         base = pl.multiple_of(step * chunk, chunk)
-        count = jnp.zeros((chunk, 1), F32)
+        tally = jnp.zeros((chunk, 256), F32)
         for g in range(groups):
             hits = (flat_ref[g] == subs_of((chunk, 256)) + base).astype(F32)
             hits_ref[g, pl.ds(base, chunk), :] = hits.astype(BF16)
-            count += jnp.sum(hits, axis=1, keepdims=True)
-        count_ref[pl.ds(base, chunk), :] = count
+            tally += hits
+        count_ref[pl.ds(base, chunk), :] = jnp.sum(tally, axis=1, keepdims=True)
         state_ref[pl.ds(base, chunk), :] = mm(mem_ref[pl.ds(base, chunk), :], ghid_ref[...])
 
+
+    slot_both = jnp.concatenate(slot_row, axis=1)
+
+    @pl.loop(0, groups)
+    def _(g):
+        placed = slot_both == subs_of((256, 2 * events)) + g * 256
+        place_ref[g] = placed.astype(F32).astype(BF16)
 
     drain(recv_sems.at[2], last_recv)
     got = jnp.concatenate(
@@ -263,31 +310,26 @@
         spread = mm(hit_col[side], got_hi) * 64.0 + mm(hit_col[side], got_lo)
         here = pos_col[side] + (me % rep) * slots == lane_e
         before = jnp.sum(jnp.where(here, spread, 0.0), axis=1, keepdims=True)
-        angle = (moment - before) * freq + phase
+        angle = (moment - before) * freq_ref[...] + phase_ref[...]
         coded.append(jnp.cos(angle).astype(BF16))
 
     drain(recv_sems.at[1], row_recv)
     fetched = row_recv[...].reshape(total, width)
     picked = []
     for side in range(2):
-        pick = (slot_col[side] == lanes_of((events, total))).astype(F32).astype(BF16)
-        picked.append(mm(pick, fetched).astype(BF16))
+        picked.append(mm(pick_ref[side], fetched).astype(BF16))
     for side in range(2):
         inputs = jnp.concatenate([picked[side], picked[1 - side], coded[side]], axis=1)
         hid = mm(inputs, win_ref[: 2 * width + time_width, :]) + edge_part
         hid = jnp.maximum(hid, 0.0).astype(BF16)
         msgs[side * events : (side + 1) * events, :] = mm(hid, wout_ref[...]).astype(BF16)
 
-    slot_both = jnp.concatenate(slot_row, axis=1)
-
-    half = groups // 2
 
     def push(first, stop, kind):
         @pl.loop(first, stop)
         def _(step):
-            g = (me // group + 1 + step) % groups
-            placed = slot_both == subs_of((256, 2 * events)) + g * 256
-            block = mm(placed.astype(F32).astype(BF16), msgs[...])
+            g = mirrored(step)
+            block = mm(place_ref[g], msgs[...])
             msg_send[pl.ds(g * group, group)] = block.astype(BF16).reshape(
                 group, slots, block.shape[1]
             )
@@ -298,8 +340,10 @@
                 def _():
                     send(kind, msg_send.at[peer], msg_recv.at[me], peer).start()
 
-    push(0, half, 3)
-    push(half, groups, 4)
+    half, quarter = groups // 2, groups // 4
+    push(0, quarter, 3)
+    push(quarter, half, 4)
+    push(half, groups, 5)
     msg_recv[pl.ds(me, 1)] = msg_send[pl.ds(me, 1)]
     drain(send_sems.at[0], req_send)
     drain(send_sems.at[1], row_send)
@@ -312,29 +356,36 @@
     def gathered(base, steps):
         acc = jnp.zeros((chunk, msgs.shape[1]), F32)
         for step in steps:
-            g = (me // group + groups - 1 - step) % groups
+            g = mirrored(step)
             block = msg_recv[pl.ds(g * group, group)].reshape(256, msgs.shape[1])
             acc += mm(hits_ref[g, pl.ds(base, chunk), :], block)
         return acc
 
-    settle(recv_sems.at[3], msg_recv, half * group)
+    settle(recv_sems.at[5], msg_recv, half * group - 1)
 
     @pl.loop(0, rows_count // chunk)
     def _(step):
         base = pl.multiple_of(step * chunk, chunk)
-        sum_ref[pl.ds(base, chunk), :] = gathered(base, range(half))
-
-    settle(recv_sems.at[4], msg_recv, half * group - 1)
+        sum_ref[pl.ds(base, chunk), :] = gathered(base, range(half, groups))
+
+    settle(recv_sems.at[3], msg_recv, quarter * group)
+
+    @pl.loop(0, rows_count // chunk)
+    def _(step):
+        base = pl.multiple_of(step * chunk, chunk)
+        sum_ref[pl.ds(base, chunk), :] += gathered(base, range(quarter))
+
+    settle(recv_sems.at[4], msg_recv, (half - quarter) * group)
 
     @pl.loop(0, rows_count // chunk)
     def _(step):
         base = pl.multiple_of(step * chunk, chunk)
         rows = pl.ds(base, chunk)
         count = count_ref[rows, :]
-        summed = sum_ref[rows, :] + gathered(base, range(half, groups))
+        summed = sum_ref[rows, :] + gathered(base, range(quarter, half))
         mean = (summed / jnp.maximum(count, 1.0)).astype(BF16)
         state = mem_ref[rows, :].astype(F32)
-        gi = mm(mean, gin_ref[...]) + gate
+        gi = mm(mean, gin_ref[...]) + bgru_ref[...]
         gh = state_ref[rows, :]
         reset = 0.5 * jnp.tanh(0.5 * (gi[:, :width] + gh[:, :width])) + 0.5
         update = 0.5 * jnp.tanh(0.5 * (gi[:, width : 2 * width] + gh[:, width : 2 * width])) + 0.5
@@ -343,8 +394,9 @@
         out_ref[rows, :] = jnp.where(count > 0.5, fresh, state).astype(BF16)
         pltpu.make_async_copy(out_ref.at[rows], out_hbm.at[rows], store_sem).start()
 
-    settle(send_sems.at[3], msg_send, half * group)
-    settle(send_sems.at[4], msg_send, half * group - 1)
+    settle(send_sems.at[3], msg_send, quarter * group)
+    settle(send_sems.at[4], msg_send, (half - quarter) * group)
+    settle(send_sems.at[5], msg_send, half * group - 1)
     pltpu.make_async_copy(out_ref, out_hbm, store_sem).wait()
 
 
@@ -373,20 +425,16 @@
     rows_count, width = memory.shape
     msg_width = w_msg_out.shape[1]
     total = n * slots
-    span = max(events, 3 * width, w_msg_out.shape[0], 2 * time_freq.shape[0])
-    small = [
-        src_owner[:, 0],
-        dst_owner[:, 0],
-        src_row,
-        dst_row,
-        event_time,
-        b_msg,
-        b_gru_in,
-        jnp.concatenate([time_freq, time_phase]),
-    ]
-    params = jnp.stack([jnp.pad(x.astype(F32), (0, span - x.shape[0])) for x in small])
     operands = (
-        params,
+        src_owner.reshape(1, events),
+        dst_owner.reshape(1, events),
+        src_row.reshape(1, events),
+        dst_row.reshape(1, events),
+        event_time.reshape(1, events),
+        time_freq.reshape(1, -1),
+        time_phase.reshape(1, -1),
+        b_msg.reshape(1, -1),
+        b_gru_in.reshape(1, -1),
         last_update.reshape(rows_count // LANES, LANES),
         memory,
         edge_feat,
@@ -407,6 +455,8 @@
             pltpu.VMEM((n, 1, LANES), jnp.int32),
             pltpu.VMEM((n, 1, LANES), jnp.int32),
             pltpu.VMEM((total, 1), jnp.int32),
+            pltpu.VMEM((2, events, total), BF16),
+            pltpu.VMEM((total // 256, 256, 2 * events), BF16),
             pltpu.VMEM((n * slots // LANES, 1, LANES), jnp.int32),
             pltpu.VMEM((n, 1, LANES), jnp.int32),
             pltpu.VMEM((n, slots, width), BF16),
@@ -419,13 +469,13 @@
             pltpu.VMEM((rows_count, 1), F32),
             pltpu.VMEM((rows_count, 3 * width), F32),
             pltpu.VMEM((rows_count, msg_width), F32),
-            pltpu.SemaphoreType.DMA((5,)),
-            pltpu.SemaphoreType.DMA((5,)),
+            pltpu.SemaphoreType.DMA((6,)),
+            pltpu.SemaphoreType.DMA((6,)),
             pltpu.SemaphoreType.DMA((len(operands),)),
             pltpu.SemaphoreType.DMA,
         ],
         compiler_params=pltpu.CompilerParams(
-            collective_id=0, has_side_effects=True, vmem_limit_bytes=58 * 1024 * 1024
+            collective_id=0, has_side_effects=True, vmem_limit_bytes=60 * 1024 * 1024
         ),
         name="exchange",
     )(*operands)

time: 88.1 us -> 77.8 us (0.88)
  the two profiles are of different devices: /device:TPU:31 before, /device:TPU:0 now
where the time goes in v3:
time: 77.8 us; the launch traced here: 77.6 us
  Pallas kernels  73.3 us (94%)
  local copies, waits for them, and re-layouts  4.31 us (6%)
    pallas_call x1, Pallas kernels, local(): pl.pallas_call(functools.partial(exchange_kernel, n, per_row, slots, even...  73.3 us
    unnamed x1, local copies, waits for them, and re-layouts  3.05 us

profile of v3, /device:TPU:0, one launch (start us, length us, event | category | flops | bytes accessed | tf_op | source)
XLA Modules:
  0.0 77.6 jit_solution(8924030019878778453)
XLA Ops:
  0.0 1.3 %reshape.38.bgru_hbm = f32[1,768]{1,0:T(1,128)} reshape(f32[768]{0:T(1024)} %param.30) | data formatting | bytes 6144 | tf_op jit(solution)/shard_map/reshape | solution.py:437
  1.3 73.3 %exchange.1 = bf16[4096,256]{1,0:T(8,128)(2,1)} custom-call(s32[1,512]{1,0:T(1,128)} %bitcast.10, s32[1,512]{1,0:T(1,128)} %bitcast.11, s32[1,512]{1,0:T(1,128)} %bitcast.12, s32[1,512]{1,0:T(1,128)} %bitcast.13, s32[1,512]{1,0:T(1,128)} %bitcast.14, f32[1,128]{1,0:T(1,128)} %bitcast.16, f32[1,128]{1,0:T(1,128)} %bitcast.17, f32[1,512]{1,0:T(1,128)} %bitcast.15, ...), custom_call_target="tpu_custom_call" | custom-call | tf_op jit(solution)/shard_map/exchange/pallas_call | solution.py:447
  74.5 3.0 %copy.18 = bf16[4096,256]{1,0:T(8,128)(2,1)} copy(bf16[4096,256]{1,0:T(8,128)(2,1)} %exchange.1) | data formatting | bytes 4194304

commit v4 on v3

--- a/solution.py
+++ b/solution.py
@@ -70,6 +70,7 @@
     rows_col,
     pick_ref,
     place_ref,
+    pick_sum,
     last_send,
     last_recv,
     row_send,
@@ -79,7 +80,7 @@
     msgs,
     flat_ref,
     hits_ref,
-    count_ref,
+    scale_ref,
     state_ref,
     sum_ref,
     send_sems,
@@ -100,6 +101,9 @@
     def coords(device):
         return (device // per_row, device % per_row)
 
+    half = groups // 2
+    quarter = half - 1
+
     def mirrored(step):
         k = (step + groups // 2) % groups
         k = k + (step // (groups // 2)) * (groups // 2 - 1 - 2 * k)
@@ -110,12 +114,6 @@
         return g
 
     barrier = pltpu.get_barrier_semaphore()
-
-    @pl.loop(1, n)
-    def _(step):
-        pl.semaphore_signal(
-            barrier, inc=1, device_id=coords((me + step) % n), device_id_type=MESH
-        )
 
     loads = [
         pltpu.make_async_copy(src, dst, load_sems.at[k])
@@ -142,6 +140,12 @@
     ]
     for load in loads:
         load.start()
+    @pl.loop(1, n)
+    def _(step):
+        pl.semaphore_signal(
+            barrier, inc=1, device_id=coords((me + step) % n), device_id_type=MESH
+        )
+
     for load in loads[:5]:
         load.wait()
     ints = jnp.concatenate(
@@ -208,7 +212,7 @@
     for side in range(2):
         for g in range(groups):
             near = slot_col[side] == lanes_of((events, 256)) + g * 256
-            pick_ref[side, :, g * 256 : (g + 1) * 256] = near.astype(F32).astype(BF16)
+            pick_ref[g, side * events : (side + 1) * events, :] = near.astype(F32).astype(BF16)
 
     req_recv[pl.ds(me, 1)] = req_send[pl.ds(me, 1)]
     drain(recv_sems.at[0], req_recv)
@@ -234,7 +238,7 @@
     for load in loads[5:]:
         load.wait()
 
-    def serve(step):
+    def serve(kind, step):
         g = mirrored(step)
         wanted = rows_col[pl.ds(pl.multiple_of(g * 256, 256), 256), :]
         acc = jnp.zeros((256, width), F32)
@@ -248,9 +252,9 @@
 
             @pl.when(peer != me)
             def _():
-                send(1, row_send.at[peer], row_recv.at[me], peer).start()
-
-    serve(0)
+                send(kind, row_send.at[peer], row_recv.at[me], peer).start()
+
+    serve(1, 0)
     last = last_ref[...]
     high_count = rows_count // LANES
     last_hi = (last // 64).astype(F32)
@@ -270,7 +274,8 @@
         peer = (me + step) % n
         send(2, last_send.at[peer // rep], last_recv.at[me], peer).start()
 
-    pl.loop(1, groups)(serve)
+    pl.loop(1, half)(functools.partial(serve, 1))
+    pl.loop(half, groups)(functools.partial(serve, 6))
     last_recv[pl.ds(me, 1)] = last_send[pl.ds(me // rep, 1)]
     row_recv[pl.ds(me, 1)] = row_send[pl.ds(me, 1)]
 
@@ -285,7 +290,8 @@
             hits = (flat_ref[g] == subs_of((chunk, 256)) + base).astype(F32)
             hits_ref[g, pl.ds(base, chunk), :] = hits.astype(BF16)
             tally += hits
-        count_ref[pl.ds(base, chunk), :] = jnp.sum(tally, axis=1, keepdims=True)
+        count = jnp.sum(tally, axis=1, keepdims=True)
+        scale_ref[pl.ds(base, chunk), :] = jnp.where(count > 0.5, 1.0 / jnp.maximum(count, 1.0), -1.0)
         state_ref[pl.ds(base, chunk), :] = mm(mem_ref[pl.ds(base, chunk), :], ghid_ref[...])
 
 
@@ -313,11 +319,23 @@
         angle = (moment - before) * freq_ref[...] + phase_ref[...]
         coded.append(jnp.cos(angle).astype(BF16))
 
-    drain(recv_sems.at[1], row_recv)
-    fetched = row_recv[...].reshape(total, width)
-    picked = []
-    for side in range(2):
-        picked.append(mm(pick_ref[side], fetched).astype(BF16))
+    def settle(sem, buf, blocks_moved):
+        part = buf.at[pl.ds(0, blocks_moved)]
+        pltpu.make_async_copy(part, part, sem).wait()
+
+    def chosen(steps):
+        acc = jnp.zeros((2 * events, width), F32)
+        for step in steps:
+            g = mirrored(step)
+            block = row_recv[pl.ds(g * group, group)].reshape(256, width)
+            acc += mm(pick_ref[g], block)
+        return acc
+
+    settle(recv_sems.at[6], row_recv, half * group - 1)
+    pick_sum[...] = chosen(range(half, groups))
+    settle(recv_sems.at[1], row_recv, half * group)
+    both = (pick_sum[...] + chosen(range(half))).astype(BF16)
+    picked = [both[:events], both[events:]]
     for side in range(2):
         inputs = jnp.concatenate([picked[side], picked[1 - side], coded[side]], axis=1)
         hid = mm(inputs, win_ref[: 2 * width + time_width, :]) + edge_part
@@ -340,18 +358,14 @@
                 def _():
                     send(kind, msg_send.at[peer], msg_recv.at[me], peer).start()
 
-    half, quarter = groups // 2, groups // 4
     push(0, quarter, 3)
     push(quarter, half, 4)
     push(half, groups, 5)
     msg_recv[pl.ds(me, 1)] = msg_send[pl.ds(me, 1)]
     drain(send_sems.at[0], req_send)
-    drain(send_sems.at[1], row_send)
+    settle(send_sems.at[1], row_send, half * group)
+    settle(send_sems.at[6], row_send, half * group - 1)
     drain(send_sems.at[2], last_recv)
-
-    def settle(sem, buf, blocks_moved):
-        part = buf.at[pl.ds(0, blocks_moved)]
-        pltpu.make_async_copy(part, part, sem).wait()
 
     def gathered(base, steps):
         acc = jnp.zeros((chunk, msgs.shape[1]), F32)
@@ -381,23 +395,27 @@
     def _(step):
         base = pl.multiple_of(step * chunk, chunk)
         rows = pl.ds(base, chunk)
-        count = count_ref[rows, :]
+        scale = scale_ref[rows, :]
         summed = sum_ref[rows, :] + gathered(base, range(quarter, half))
-        mean = (summed / jnp.maximum(count, 1.0)).astype(BF16)
+        mean = (summed * scale).astype(BF16)
         state = mem_ref[rows, :].astype(F32)
-        gi = mm(mean, gin_ref[...]) + bgru_ref[...]
+        gi = mm(mean, gin_ref[...]) + bgru_ref[...].reshape(1, 3 * width)
         gh = state_ref[rows, :]
         reset = 0.5 * jnp.tanh(0.5 * (gi[:, :width] + gh[:, :width])) + 0.5
         update = 0.5 * jnp.tanh(0.5 * (gi[:, width : 2 * width] + gh[:, width : 2 * width])) + 0.5
         candid = jnp.tanh(gi[:, 2 * width :] + reset * gh[:, 2 * width :])
         fresh = candid + update * (state - candid)
-        out_ref[rows, :] = jnp.where(count > 0.5, fresh, state).astype(BF16)
+        out_ref[rows, :] = jnp.where(scale > 0.0, fresh, state).astype(BF16)
         pltpu.make_async_copy(out_ref.at[rows], out_hbm.at[rows], store_sem).start()
 
     settle(send_sems.at[3], msg_send, quarter * group)
     settle(send_sems.at[4], msg_send, (half - quarter) * group)
     settle(send_sems.at[5], msg_send, half * group - 1)
     pltpu.make_async_copy(out_ref, out_hbm, store_sem).wait()
+
+
+def hand_over_kernel(in_ref, out_ref):
+    out_ref[...] = in_ref[...]
 
 
 def local(
@@ -434,7 +452,7 @@
         time_freq.reshape(1, -1),
         time_phase.reshape(1, -1),
         b_msg.reshape(1, -1),
-        b_gru_in.reshape(1, -1),
+        b_gru_in,
         last_update.reshape(rows_count // LANES, LANES),
         memory,
         edge_feat,
@@ -444,7 +462,7 @@
         w_gru_hid,
     )
     anywhere = pl.BlockSpec(memory_space=pl.ANY)
-    return pl.pallas_call(
+    result = pl.pallas_call(
         functools.partial(exchange_kernel, n, per_row, slots, events, time_freq.shape[0]),
         out_shape=jax.ShapeDtypeStruct(memory.shape, BF16),
         in_specs=[anywhere] * len(operands),
@@ -455,8 +473,9 @@
             pltpu.VMEM((n, 1, LANES), jnp.int32),
             pltpu.VMEM((n, 1, LANES), jnp.int32),
             pltpu.VMEM((total, 1), jnp.int32),
-            pltpu.VMEM((2, events, total), BF16),
+            pltpu.VMEM((total // 256, 2 * events, 256), BF16),
             pltpu.VMEM((total // 256, 256, 2 * events), BF16),
+            pltpu.VMEM((2 * events, width), F32),
             pltpu.VMEM((n * slots // LANES, 1, LANES), jnp.int32),
             pltpu.VMEM((n, 1, LANES), jnp.int32),
             pltpu.VMEM((n, slots, width), BF16),
@@ -469,8 +488,8 @@
             pltpu.VMEM((rows_count, 1), F32),
             pltpu.VMEM((rows_count, 3 * width), F32),
             pltpu.VMEM((rows_count, msg_width), F32),
-            pltpu.SemaphoreType.DMA((6,)),
-            pltpu.SemaphoreType.DMA((6,)),
+            pltpu.SemaphoreType.DMA((7,)),
+            pltpu.SemaphoreType.DMA((7,)),
             pltpu.SemaphoreType.DMA((len(operands),)),
             pltpu.SemaphoreType.DMA,
         ],
@@ -479,6 +498,16 @@
         ),
         name="exchange",
     )(*operands)
+    part = pl.BlockSpec((min(1024, rows_count), width), lambda i: (i, 0))
+    return pl.pallas_call(
+        hand_over_kernel,
+        grid=(rows_count // min(1024, rows_count),),
+        out_shape=jax.ShapeDtypeStruct(memory.shape, BF16),
+        in_specs=[part],
+        out_specs=part,
+        compiler_params=pltpu.CompilerParams(vmem_limit_bytes=60 * 1024 * 1024),
+        name="hand_over",
+    )(result)
 
 
 def solution(mesh):

time: 77.8 us -> 78.2 us (level)
  Pallas kernels: 73.3 us -> 78 us
  local copies, waits for them, and re-layouts: 4.31 us -> 0 us
    pallas_call x0 -> x1, Pallas kernels: none -> 3.78 us  [local(): pl.pallas_call(hand_over_kernel, grid=(rows_count // min(1024, rows_count...]
    unnamed x1 -> x0, local copies, waits for them, and re-layouts: 3.05 us -> none
    reshape x1 -> x0, local copies, waits for them, and re-layouts: 1.27 us -> none  [local(): b_gru_in.reshape(1, -1)]
    pallas_call x1, Pallas kernels: 73.3 us -> 74.2 us  [local(): pl.pallas_call(functools.partial(exchange_kernel, n, per_row, slots, even...]
where the time goes in v4:
time: 78.2 us; the launch traced here: 78 us
  Pallas kernels  78 us (100%)
    pallas_call x1, Pallas kernels, local(): pl.pallas_call(functools.partial(exchange_kernel, n, per_row, slots, even...  74.2 us
    pallas_call x1, Pallas kernels, local(): pl.pallas_call(hand_over_kernel, grid=(rows_count // min(1024, rows_count...  3.78 us

profile of v4, /device:TPU:0, one launch (start us, length us, event | category | flops | bytes accessed | tf_op | source)
XLA Modules:
  0.0 78.0 jit_solution(11658456666574834015)
XLA Ops:
  0.0 74.2 %exchange.1.in_ref = bf16[4096,256]{1,0:T(8,128)(2,1)} custom-call(s32[1,512]{1,0:T(1,128)} %bitcast.10, s32[1,512]{1,0:T(1,128)} %bitcast.11, s32[1,512]{1,0:T(1,128)} %bitcast.12, s32[1,512]{1,0:T(1,128)} %bitcast.13, s32[1,512]{1,0:T(1,128)} %bitcast.14, f32[1,128]{1,0:T(1,128)} %bitcast.16, f32[1,128]{1,0:T(1,128)} %bitcast.17, f32[1,512]{1,0:T(1,128)} %bitcast.15, ...), custom_call_target="tpu_custom_call" | custom-call | tf_op jit(solution)/shard_map/exchange/pallas_call | solution.py:465
  74.2 3.8 %hand_over.1 = bf16[4096,256]{1,0:T(8,128)(2,1)} custom-call(bf16[4096,256]{1,0:T(8,128)(2,1)} %exchange.1.in_ref), custom_call_target="tpu_custom_call" | custom-call | tf_op jit(solution)/shard_map/hand_over/pallas_call | solution.py:502

commit v5 on v4

--- a/solution.py
+++ b/solution.py
@@ -285,13 +285,6 @@
     @pl.loop(0, rows_count // chunk)
     def _(step):
         base = pl.multiple_of(step * chunk, chunk)
-        tally = jnp.zeros((chunk, 256), F32)
-        for g in range(groups):
-            hits = (flat_ref[g] == subs_of((chunk, 256)) + base).astype(F32)
-            hits_ref[g, pl.ds(base, chunk), :] = hits.astype(BF16)
-            tally += hits
-        count = jnp.sum(tally, axis=1, keepdims=True)
-        scale_ref[pl.ds(base, chunk), :] = jnp.where(count > 0.5, 1.0 / jnp.maximum(count, 1.0), -1.0)
         state_ref[pl.ds(base, chunk), :] = mm(mem_ref[pl.ds(base, chunk), :], ghid_ref[...])
 
 
@@ -375,6 +368,17 @@
             acc += mm(hits_ref[g, pl.ds(base, chunk), :], block)
         return acc
 
+    @pl.loop(0, rows_count // chunk)
+    def _(step):
+        base = pl.multiple_of(step * chunk, chunk)
+        tally = jnp.zeros((chunk, 256), F32)
+        for g in range(groups):
+            hits = (flat_ref[g] == subs_of((chunk, 256)) + base).astype(F32)
+            hits_ref[g, pl.ds(base, chunk), :] = hits.astype(BF16)
+            tally += hits
+        count = jnp.sum(tally, axis=1, keepdims=True)
+        scale_ref[pl.ds(base, chunk), :] = jnp.where(count > 0.5, 1.0 / jnp.maximum(count, 1.0), -1.0)
+
     settle(recv_sems.at[5], msg_recv, half * group - 1)
 
     @pl.loop(0, rows_count // chunk)
@@ -412,10 +416,6 @@
     settle(send_sems.at[4], msg_send, (half - quarter) * group)
     settle(send_sems.at[5], msg_send, half * group - 1)
     pltpu.make_async_copy(out_ref, out_hbm, store_sem).wait()
-
-
-def hand_over_kernel(in_ref, out_ref):
-    out_ref[...] = in_ref[...]
 
 
 def local(
@@ -462,7 +462,7 @@
         w_gru_hid,
     )
     anywhere = pl.BlockSpec(memory_space=pl.ANY)
-    result = pl.pallas_call(
+    return pl.pallas_call(
         functools.partial(exchange_kernel, n, per_row, slots, events, time_freq.shape[0]),
         out_shape=jax.ShapeDtypeStruct(memory.shape, BF16),
         in_specs=[anywhere] * len(operands),
@@ -498,16 +498,6 @@
         ),
         name="exchange",
     )(*operands)
-    part = pl.BlockSpec((min(1024, rows_count), width), lambda i: (i, 0))
-    return pl.pallas_call(
-        hand_over_kernel,
-        grid=(rows_count // min(1024, rows_count),),
-        out_shape=jax.ShapeDtypeStruct(memory.shape, BF16),
-        in_specs=[part],
-        out_specs=part,
-        compiler_params=pltpu.CompilerParams(vmem_limit_bytes=60 * 1024 * 1024),
-        name="hand_over",
-    )(result)
 
 
 def solution(mesh):

time: 78.2 us -> 77.4 us (0.990)
  Pallas kernels: 78 us -> 74.2 us
  local copies, waits for them, and re-layouts: 0 us -> 3.05 us
    pallas_call x1 -> x0, Pallas kernels: 3.78 us -> none  [local(): pl.pallas_call(hand_over_kernel, grid=(rows_count // min(1024, rows_count...]
    unnamed x0 -> x1, local copies, waits for them, and re-layouts: none -> 3.05 us
where the time goes in v5:
time: 77.4 us; the launch traced here: 77.3 us
  Pallas kernels  74.2 us (96%)
  local copies, waits for them, and re-layouts  3.05 us (4%)
    pallas_call x1, Pallas kernels, local(): pl.pallas_call(functools.partial(exchange_kernel, n, per_row, slots, even...  74.2 us
    unnamed x1, local copies, waits for them, and re-layouts  3.05 us

profile of v5, /device:TPU:0, one launch (start us, length us, event | category | flops | bytes accessed | tf_op | source)
XLA Modules:
  0.0 77.3 jit_solution(14874720910963814871)
XLA Ops:
  0.0 74.2 %exchange.1 = bf16[4096,256]{1,0:T(8,128)(2,1)} custom-call(s32[1,512]{1,0:T(1,128)} %bitcast.10, s32[1,512]{1,0:T(1,128)} %bitcast.11, s32[1,512]{1,0:T(1,128)} %bitcast.12, s32[1,512]{1,0:T(1,128)} %bitcast.13, s32[1,512]{1,0:T(1,128)} %bitcast.14, f32[1,128]{1,0:T(1,128)} %bitcast.16, f32[1,128]{1,0:T(1,128)} %bitcast.17, f32[1,512]{1,0:T(1,128)} %bitcast.15, ...), custom_call_target="tpu_custom_call" | custom-call | tf_op jit(solution)/shard_map/exchange/pallas_call | solution.py:465
  74.2 3.0 %copy.18 = bf16[4096,256]{1,0:T(8,128)(2,1)} copy(bf16[4096,256]{1,0:T(8,128)(2,1)} %exchange.1) | data formatting | bytes 4194304

commit v6 on v5

--- a/solution.py
+++ b/solution.py
@@ -105,8 +105,8 @@
     quarter = half - 1
 
     def mirrored(step):
-        k = (step + groups // 2) % groups
-        k = k + (step // (groups // 2)) * (groups // 2 - 1 - 2 * k)
+        far, near = half + (step + half // 2) % half, groups - 1 - step
+        k = far + (step // half) * (near - far)
         g, unit = 0, 1
         while unit < groups:
             g = g + unit * ((me // group // unit + k // unit) % 2)

time: 77.4 us -> 76.2 us (0.984)
  the two profiles are of different devices: /device:TPU:0 before, /device:TPU:9 now
where the time goes in v6:
time: 76.2 us; the launch traced here: 76 us
  Pallas kernels  72.9 us (96%)
  local copies, waits for them, and re-layouts  3.05 us (4%)
    pallas_call x1, Pallas kernels, local(): pl.pallas_call(functools.partial(exchange_kernel, n, per_row, slots, even...  72.9 us
    unnamed x1, local copies, waits for them, and re-layouts  3.05 us

profile of v6, /device:TPU:9, one launch (start us, length us, event | category | flops | bytes accessed | tf_op | source)
XLA Modules:
  0.0 76.0 jit_solution(3631348003324501116)
XLA Ops:
  0.0 72.9 %exchange.1 = bf16[4096,256]{1,0:T(8,128)(2,1)} custom-call(s32[1,512]{1,0:T(1,128)} %bitcast.10, s32[1,512]{1,0:T(1,128)} %bitcast.11, s32[1,512]{1,0:T(1,128)} %bitcast.12, s32[1,512]{1,0:T(1,128)} %bitcast.13, s32[1,512]{1,0:T(1,128)} %bitcast.14, f32[1,128]{1,0:T(1,128)} %bitcast.16, f32[1,128]{1,0:T(1,128)} %bitcast.17, f32[1,512]{1,0:T(1,128)} %bitcast.15, ...), custom_call_target="tpu_custom_call" | custom-call | tf_op jit(solution)/shard_map/exchange/pallas_call | solution.py:465
  73.0 3.0 %copy.18 = bf16[4096,256]{1,0:T(8,128)(2,1)} copy(bf16[4096,256]{1,0:T(8,128)(2,1)} %exchange.1) | data formatting | bytes 4194304
